TPU v7x, 32 devices: a whole 2x2x4 slice. The times are simulated.
32 devices in a mesh: group: 2 (over y), fsdp: 4 (over z), tensor: 4 (over x, core).
Axes of the slice: x: 2, y: 2, z: 4, core: 2. Of those that a mesh axis runs over, the one named last changes fastest.
Arguments:
- inputs: bfloat16 [1536, 8192], P(('group', 'fsdp'), 'tensor'), parts along dimension 0, may hold values from -3 to 3
- grad_out: bfloat16 [1536, 28672], P(('group', 'tensor'), 'fsdp'), parts along dimension 0, may hold values from -6 to 6
- base_weight: bfloat16 [8192, 28672], P('tensor', 'fsdp'), may hold values from -0.03125 to 0.03125
- factor_a: bfloat16 [6, 8192, 64], P(None, ('tensor', 'fsdp')), may hold values from -0.1875 to 0.1875
- factor_b: bfloat16 [6, 64, 28672], P(None, None, 'fsdp'), may hold values from -0.03125 to 0.03125
- group_adapter: int32 [16], P('group'), parts along dimension 0, may hold values from 0 to 5
- group_len: int32 [16], P('group'), parts along dimension 0, may hold values from 1 to 96, 576 in all
Outputs:
- input_grad: bfloat16 [1536, 8192], P(('group', 'fsdp'), 'tensor'), parts along dimension 0
- grad_a: float32 [12, 8192, 64], P('group', ('tensor', 'fsdp')), parts along dimension 0
- grad_b: bfloat16 [12, 64, 28672], P('group', None, 'fsdp'), parts along dimension 0
There are 2 independent parts, one for each index of `group`. A program takes and returns all parts, laid end to end along the dimension named above; an argument that names none is the same for every part. Nothing has to cross between parts.
Inputs may be any that keep to these rules, and one draw needn't show every extreme that they name: `group_adapter`: group g is hosted by index g // 2 of fsdp; an adapter may have several groups. `group_len`: rows of a group past its length are padding; some group is full.
All inputs are finite; a program needn't handle non-finite values.
Results may differ from a plain program's by a relative error of at most 0.011.
Values may be sent and summed in bfloat16 or wider, within the bound.
A program may use at most 128 MiB of HBM per device.

v0:
```python
import jax
import jax.numpy as jnp
from jax import lax
from jax.sharding import PartitionSpec as P

GPD = 2


def body(inputs, grad_out, base_weight, factor_a, factor_b, group_adapter, group_len):
    host_rows, feature_cols = inputs.shape
    slot_rows = host_rows // GPD
    owner_index = lax.axis_index("fsdp")
    adapters = factor_b.shape[0]
    rank_dim = factor_b.shape[1]
    hidden_cols = factor_b.shape[2]
    gathered = lax.all_gather(grad_out, "tensor", axis=0, tiled=True)
    total_rows = gathered.shape[0]
    row_index = jnp.arange(total_rows, dtype=jnp.int32)
    adapter_row = jnp.repeat(group_adapter, slot_rows)
    length_row = jnp.repeat(group_len, slot_rows)
    row_valid = (row_index % slot_rows < length_row).astype(jnp.float32)
    member = (adapter_row[:, None] == jnp.arange(adapters, dtype=jnp.int32)[None, :]).astype(
        jnp.float32
    ) * row_valid[:, None]
    b_flat = factor_b.reshape(adapters * rank_dim, hidden_cols)
    grad_every = lax.dot_general(
        gathered, b_flat, (((1,), (1,)), ((), ())), preferred_element_type=jnp.float32
    )
    grad_part = jnp.sum(
        grad_every.reshape(total_rows, adapters, rank_dim) * member[:, :, None], axis=1
    )
    low_grad = lax.psum_scatter(grad_part, "fsdp", scatter_dimension=0, tiled=True)
    base_term = lax.psum_scatter(
        lax.dot_general(
            gathered, base_weight, (((1,), (1,)), ((), ())), preferred_element_type=jnp.float32
        ),
        "fsdp",
        scatter_dimension=0,
        tiled=True,
    )
    host_list = lax.dynamic_slice_in_dim(group_adapter, owner_index * GPD, GPD)
    host_member = host_list[:, None] == jnp.arange(adapters, dtype=jnp.int32)[None, :]
    host_pick = host_member.astype(jnp.bfloat16)
    picked = jnp.einsum(
        "ga,adr->gdr",
        host_pick,
        lax.all_gather(factor_a, "fsdp", axis=1, tiled=True),
        preferred_element_type=jnp.float32,
    ).astype(jnp.bfloat16)
    input_groups = inputs.reshape(GPD, slot_rows, feature_cols)
    input_part = jnp.einsum(
        "gsd,gdr->gsr", input_groups, picked, preferred_element_type=jnp.float32
    )
    low_in = lax.psum(input_part, "tensor")
    host_valid = lax.dynamic_slice_in_dim(row_valid, owner_index * host_rows, host_rows).reshape(
        GPD, slot_rows
    )
    low_in_b = (low_in * host_valid[:, :, None]).astype(jnp.bfloat16)
    low_grad_b = low_grad.astype(jnp.bfloat16).reshape(GPD, slot_rows, rank_dim)
    low_rank = jnp.einsum("gsr,gdr->gsd", low_grad_b, picked, preferred_element_type=jnp.float32)
    input_grad = (base_term + low_rank.reshape(host_rows, feature_cols)).astype(jnp.bfloat16)
    host_grad = jnp.einsum(
        "gsd,gsr->gdr", input_groups, low_grad_b, preferred_element_type=jnp.float32
    )
    spread_grad = jnp.einsum(
        "ga,gdr->adr", host_member.astype(jnp.float32), host_grad, precision=lax.Precision.HIGHEST
    )
    grad_a = lax.psum_scatter(spread_grad, "fsdp", scatter_dimension=1, tiled=True)
    all_inputs = lax.all_gather(low_in_b.reshape(host_rows, rank_dim), "fsdp", axis=0, tiled=True)
    spread_in = (member.astype(jnp.bfloat16)[:, :, None] * all_inputs[:, None, :]).reshape(
        total_rows, adapters * rank_dim
    )
    grad_flat = lax.dot_general(
        spread_in, gathered, (((0,), (0,)), ((), ())), preferred_element_type=jnp.float32
    )
    grad_b = grad_flat.reshape(adapters, rank_dim, hidden_cols).astype(jnp.bfloat16)
    return (input_grad, grad_a, grad_b)


def solution(mesh):
    placed = (
        P(("group", "fsdp"), "tensor"),
        P(("group", "tensor"), "fsdp"),
        P("tensor", "fsdp"),
        P(None, ("tensor", "fsdp"), None),
        P(None, None, "fsdp"),
        P("group"),
        P("group"),
    )
    return jax.shard_map(
        body,
        mesh=mesh,
        in_specs=placed,
        out_specs=(
            P(("group", "fsdp"), "tensor"),
            P("group", ("tensor", "fsdp"), None),
            P("group", None, "fsdp"),
        ),
        check_vma=False,
    )
```

profile of v0, /device:TPU:0, one launch (start us, length us, event | category | flops | bytes accessed | tf_op | source)
XLA Modules:
  0.0 366.1 jit_solution(11815815997242455206)
XLA Ops:
  7.2 0.7 all-gather.4.cloned.1.call-update
  8.0 0.7 broadcast_in_dim.5
  8.8 0.7 broadcast_in_dim.4
  9.6 75.9 %all-gather.4.cloned.1.call-done = bf16[768,7168]{1,0:T(8,128)(2,1)} async-done(((bf16[192,7168]{1,0:T(8,128)(2,1)}), bf16[768,7168]{1,0:T(8,128)(2,1)}) %all-gather.4.cloned.1.call-update) | async-done | bytes 11010064 | tf_op jit(solution)/shard_map/all_gather | solution.py:16
  85.5 10.2 %fusion.11 = f32[768,64]{0,1:T(8,128)S(1)} fusion(bf16[6,64,7168]{2,1,0:T(8,128)(2,1)} %param.11, bf16[768,7168]{1,0:T(8,128)(2,1)} %all-gather.4.cloned.1.call-done, f32[768,6]{0,1:T(8,128)S(1)} %fusion.25), kind=kOutput, calls=%fused_computation.10 | convolution fusion | flops 4228399104 | bytes 16730112 | tf_op jit(solution)/shard_map/dot_general | solution.py:26
  95.6 0.9 copy.38
  96.6 1.0 copy.29
  97.8 19.5 %reduce-scatter.10.cloned.1.call-done = f32[192,64]{1,0:T(8,128)} async-done(((f32[768,64]{1,0:T(8,128)}), f32[192,64]{1,0:T(8,128)}) %reduce-scatter.10.cloned.1.call-update) | async-done | bytes 49168
  117.3 1.0 copy.39
  118.4 0.3 convolution_bitcast_fusion
  118.7 4.4 %fusion.14 = f32[6,2048,64]{1,0,2:T(8,128)} fusion(f32[2,2048,64]{1,2,0:T(8,128)S(1)} %convolution_bitcast_fusion, s32[2]{0:T(128)S(1)} %dynamic_slice.6), kind=kOutput, calls=%fused_computation.12 | convolution fusion | flops 18874380 | bytes 4194312 | tf_op jit(solution)/shard_map/ga,gdr->adr/dot_general | solution.py:65
  123.1 0.2 reduce-scatter.6.cloned.1.call-start
  123.4 31.4 %fusion.36 = f32[768,2048]{1,0:T(8,128)} fusion(bf16[768,7168]{1,0:T(8,128)(2,1)} %all-gather.4.cloned.1.call-done, bf16[2048,7168]{1,0:T(8,128)(2,1)} %param.9), kind=kOutput, calls=%fused_computation.39 | convolution fusion | flops 22548578304 | bytes 46661632 | tf_op jit(solution)/shard_map/dot_general | solution.py:34
  155.0 8.8 %all-gather.6.cloned.1.call-done = bf16[6,2048,64]{1,0,2:T(8,128)(2,1)} async-done(((bf16[6,512,64]{1,0,2:T(8,128)(2,1)}), bf16[6,2048,64]{1,0,2:T(8,128)(2,1)}) %all-gather.6.cloned.1.call-update) | async-done | bytes 1572880 | tf_op jit(solution)/shard_map/all_gather | solution.py:47
  163.8 2.3 convolution_convert_fusion
  166.2 0.4 convolution_bitcast_fusion.1
  166.6 12.3 %psum.7 = f32[2,96,64]{1,2,0:T(8,128)S(1)} all-reduce(f32[2,96,64]{1,2,0:T(8,128)S(1)} %convolution_bitcast_fusion.1), channel_id=1, replica_groups=mesh['group'=2,'fsdp'=4,'tensor'=4] {'tensor'}, use_global_device_ids=true, to_apply=%region_4.5 | all-reduce | flops 12288 | bytes 98304 | tf_op jit(solution)/shard_map/psum | solution.py:54
  179.1 14.5 %all-gather = bf16[4,192,64]{1,2,0:T(8,128)(2,1)S(1)} all-gather(bf16[1,192,64]{1,2,0:T(8,128)(2,1)S(1)} %reshape.129), channel_id=1, replica_groups=mesh['group'=2,'fsdp'=4,'tensor'=4] {'fsdp'}, dimensions={0}, use_global_device_ids=true | all-gather | bytes 122880 | tf_op jit(solution)/shard_map/all_gather | solution.py:69
  193.8 10.3 %fusion.4 = bf16[6,64,7168]{2,1,0:T(8,128)(2,1)} fusion(bf16[768,7168]{1,0:T(8,128)(2,1)} %all-gather.4.cloned.1.call-done, bf16[768,64]{0,1:T(8,128)(2,1)S(1)} %reshape.130, bf16[768,6]{0,1:T(8,128)(2,1)S(1)} %fusion.31), kind=kOutput, calls=%fused_computation.4 | convolution fusion | flops 4230905856 | bytes 16622592 | tf_op jit(solution)/shard_map/dot_general | solution.py:73
  204.1 0.5 fusion.19
  204.6 39.1 %reduce-scatter.8.cloned.1.call-done = f32[6,512,64]{1,0,2:T(8,128)} async-done(((f32[6,2048,64]{1,0,2:T(8,128)}), f32[6,512,64]{1,0,2:T(8,128)}) %reduce-scatter.8.cloned.1.call-update) | async-done | bytes 786448 | tf_op jit(solution)/shard_map/reduce_scatter | solution.py:68
  243.7 2.6 copy.37
  246.2 110.8 %reduce-scatter.6.cloned.1.call-done = f32[192,2048]{1,0:T(8,128)} async-done(((f32[768,2048]{1,0:T(8,128)}), f32[192,2048]{1,0:T(8,128)}) %reduce-scatter.6.cloned.1.call-update) | async-done | bytes 1572880 | tf_op jit(solution)/shard_map/reduce_scatter | solution.py:33
  357.1 2.5 fusion.7
  (28 shorter events, 1.1 us)
Async XLA Ops:
  7.2 111.2 %copy-start = (bf16[192,2048]{1,0:T(8,128)(2,1)S(1)}, bf16[192,2048]{1,0:T(8,128)(2,1)}, u32[]{:S(2)}) copy-start(bf16[192,2048]{1,0:T(8,128)(2,1)} %param.7) | copy-start | bytes 2359300
  7.2 78.3 %all-gather.4.cloned.1.call-start = ((), (), s32[]{:S(2)}) async-start(), calls=%async_computation.3 | async-start | bytes 13762560 | tf_op jit(solution)/shard_map/all_gather | solution.py:16
  7.9 109.4 %reduce-scatter.10.cloned.1.call-start = ((), (), s32[]{:S(2)}) async-start(), calls=%async_computation.7 | async-start | bytes 491520
  9.6 87.1 %copy-start.1 = (bf16[6,512,64]{1,2,0:T(8,128)(2,1)S(1)}, bf16[6,512,64]{1,2,0:T(8,128)(2,1)}, u32[]{:S(2)}) copy-start(bf16[6,512,64]{1,2,0:T(8,128)(2,1)} %param.10) | copy-start | bytes 1179652
  9.6 88.1 %copy-start.2 = (s32[8]{0:T(128)S(1)}, s32[8]{0:T(128)}, u32[]{:S(2)}) copy-start(s32[8]{0:T(128)} %param.12) | copy-start | bytes 100
  96.6 67.2 %all-gather.6.cloned.1.call-start = ((), (), s32[]{:S(2)}) async-start(), calls=%async_computation.5 | async-start | bytes 2621440 | tf_op jit(solution)/shard_map/all_gather | solution.py:47
  97.7 146.0 %reduce-scatter.8.cloned.1.call-start = ((), (), s32[]{:S(2)}) async-start(), calls=%async_computation.6 | async-start | bytes 5242880 | tf_op jit(solution)/shard_map/reduce_scatter | solution.py:68
  123.1 234.0 %reduce-scatter.6.cloned.1.call-start = ((), (), s32[]{:S(2)}) async-start(), calls=%async_computation.4 | async-start | bytes 7864320 | tf_op jit(solution)/shard_map/reduce_scatter | solution.py:33
Sparse Core Ops, SparseCore 0:
  9.6 75.8 all-gather.3
  96.7 20.5 reduce-scatter.9
  119.6 44.2 all-gather.5
  166.1 77.5 reduce-scatter.7
  245.8 111.2 reduce-scatter.5
where the time goes:
time: 366 us
  waiting for transfers between devices  255 us (70%)
  matrix products  59.8 us (16%)
  blocking collectives  26.8 us (7%)
  between operations  13.9 us (4%)
  local copies, waits for them, and re-layouts  7.77 us (2%)
    reduce_scatter x1, waiting for transfers between devices, body(): lax.psum_scatter(lax.dot_general(gathered, base_weight, (((1,), (1,)), ((...  111 us
    all_gather x1, waiting for transfers between devices, body(): gathered = lax.all_gather(grad_out, 'tensor', axis=0, tiled=True)  75.9 us
    reduce_scatter x1, waiting for transfers between devices, body(): lax.psum_scatter(spread_grad, 'fsdp', scatter_dimension=1, tiled=True)  39.1 us
    dot_general x1, matrix products, body(): lax.dot_general(gathered, base_weight, (((1,), (1,)), ((), ())), preferre...  31.4 us
    unnamed x6, waiting for transfers between devices  20.3 us
    all_gather x1, blocking collectives, body(): lax.all_gather(low_in_b.reshape(host_rows, rank_dim), 'fsdp', axis=0, til...  14.5 us
    psum x1, blocking collectives, body(): low_in = lax.psum(input_part, 'tensor')  12.3 us
    dot_general x1, matrix products, body(): lax.dot_general(spread_in, gathered, (((0,), (0,)), ((), ())), preferred_...  10.3 us
  transfers between devices with their start and end apart: 5, of which 5 were waited for; matrix products, arithmetic and copies ran while one was open for 15% of the time, Pallas kernels for 0%

commit v1 on v0

--- a/solution.py
+++ b/solution.py
@@ -3,11 +3,9 @@
 from jax import lax
 from jax.sharding import PartitionSpec as P
 
-GPD = 2
-
-
 def body(inputs, grad_out, base_weight, factor_a, factor_b, group_adapter, group_len):
     host_rows, feature_cols = inputs.shape
+    GPD = group_adapter.shape[0] // lax.axis_size("fsdp")
     slot_rows = host_rows // GPD
     owner_index = lax.axis_index("fsdp")
     adapters = factor_b.shape[0]
@@ -77,7 +75,135 @@
     return (input_grad, grad_a, grad_b)
 
 
+def take(blocks, index):
+    return lax.dynamic_index_in_dim(blocks, index, 0, keepdims=False)
+
+
+def swap(value, axis, mask, count):
+    return lax.ppermute(value, axis, [(i, i ^ mask) for i in range(count)])
+
+
+def after(value, earlier):
+    return lax.optimization_barrier((value, earlier))[0]
+
+
+def body4(inputs, grad_out, base_weight, factor_a, factor_b, group_adapter, group_len):
+    n = 4
+    host_rows, feature_cols = inputs.shape
+    adapters, rank_dim, hidden_cols = factor_b.shape
+    own_cols = feature_cols // n
+    total_rows = host_rows * n
+    slot_rows = total_rows // group_adapter.shape[0]
+    t = lax.axis_index("tensor")
+    z = lax.axis_index("fsdp")
+    wide = adapters * rank_dim
+    chunks = 2
+    step_rows = host_rows // chunks
+    bf16, f32 = jnp.bfloat16, jnp.float32
+
+    mate = swap(grad_out, "tensor", 1, n)
+    pieces = []
+    across = None
+    for c in range(chunks):
+        sent = grad_out[c * step_rows : (c + 1) * step_rows]
+        if across is not None:
+            sent = after(sent, across)
+        across = swap(sent, "tensor", 2, n)
+        relayed = swap(across, "tensor", 1, n)
+        pieces.append((c, across, relayed))
+
+    by_owner = inputs.reshape(host_rows, n, own_cols).transpose(1, 0, 2)
+    kept = take(by_owner, z)
+    arrived = [kept] + [swap(take(by_owner, z ^ j), "fsdp", j, n) for j in range(1, n)]
+    rows_in = jnp.stack(arrived)
+
+    row_index = jnp.arange(total_rows, dtype=jnp.int32)
+    adapter_row = jnp.repeat(group_adapter, slot_rows)
+    length_row = jnp.repeat(group_len, slot_rows)
+    row_valid = (row_index % slot_rows < length_row).astype(f32)
+    member = (adapter_row[:, None] == jnp.arange(adapters, dtype=jnp.int32)[None, :]).astype(
+        f32
+    ) * row_valid[:, None]
+    member_blocks = member.reshape(n, host_rows, adapters)
+
+    def ordered(blocks, start):
+        return jnp.stack([take(blocks, start ^ j) for j in range(n)])
+
+    def pick(every, who):
+        rows = every.shape[0]
+        return jnp.sum(every.reshape(rows, adapters, rank_dim) * who[:, :, None], axis=1)
+
+    def spread(low, who):
+        rows = low.shape[0]
+        return (who.astype(bf16)[:, :, None] * low.astype(bf16)[:, None, :]).reshape(rows, wide)
+
+    b_flat = factor_b.reshape(wide, hidden_cols)
+    a_flat = jnp.transpose(factor_a, (1, 0, 2)).reshape(own_cols, wide)
+    grad_part = pick(
+        lax.dot_general(grad_out, b_flat, (((1,), (1,)), ((), ())), preferred_element_type=f32),
+        take(member_blocks, t),
+    )
+    grad_part = lax.dynamic_update_index_in_dim(
+        jnp.zeros((n, host_rows, rank_dim), f32), grad_part, t, 0
+    ).reshape(total_rows, rank_dim)
+    rows_in = ordered(rows_in, z).reshape(total_rows, own_cols)
+    in_part = pick(jnp.dot(rows_in, a_flat, preferred_element_type=f32), member)
+    low = lax.psum(jnp.concatenate([grad_part, in_part], axis=1), ("tensor", "fsdp"))
+    low_grad = low[:, :rank_dim]
+    low_in = low[:, rank_dim:]
+
+    spread_grad = spread(low_grad, member)
+    grad_a = lax.dot_general(
+        spread_grad, rows_in, (((0,), (0,)), ((), ())), preferred_element_type=f32
+    ).reshape(adapters, rank_dim, own_cols).transpose(0, 2, 1)
+    low_rank = lax.dot_general(
+        spread_grad, a_flat, (((1,), (1,)), ((), ())), preferred_element_type=f32
+    )
+    low_rank = lax.dynamic_update_slice_in_dim(
+        jnp.zeros((total_rows, feature_cols), bf16), low_rank.astype(bf16), z * own_cols, 1
+    ).reshape(n, host_rows, feature_cols)
+
+    in_order = ordered(low_in.reshape(n, host_rows, rank_dim), t)
+    member_order = ordered(member_blocks, t)
+
+    grad_b = None
+    finished = []
+    for c, across, relayed in pieces:
+        rows = slice(c * step_rows, (c + 1) * step_rows)
+        gathered = jnp.concatenate([grad_out[rows], mate[rows], across, relayed], axis=0)
+        part = lax.dot_general(
+            gathered, base_weight, (((1,), (1,)), ((), ())), preferred_element_type=f32
+        ).astype(bf16).reshape(n, step_rows, feature_cols)
+
+        def own(dest):
+            dest = jnp.clip(dest, 0, n - 1)
+            return take(part, dest ^ t).astype(f32) + take(low_rank[:, rows], dest).astype(f32)
+
+        up = down = None
+        for k in range(1, n):
+            to_up, to_down = own(z + n - k), own(z - n + k)
+            if up is not None:
+                to_up, to_down = to_up + up.astype(f32), to_down + down.astype(f32)
+            up = lax.ppermute(to_up.astype(bf16), "fsdp", [(i, i + 1) for i in range(k)])
+            down = lax.ppermute(
+                to_down.astype(bf16), "fsdp", [(n - 1 - i, n - 2 - i) for i in range(k)]
+            )
+        finished.append((own(z) + up.astype(f32) + down.astype(f32)).astype(bf16))
+
+        spread_in = spread(
+            in_order[:, rows].reshape(n * step_rows, rank_dim),
+            member_order[:, rows].reshape(n * step_rows, adapters),
+        )
+        term = lax.dot_general(
+            spread_in, gathered, (((0,), (0,)), ((), ())), preferred_element_type=f32
+        )
+        grad_b = term if grad_b is None else grad_b + term
+    grad_b = grad_b.astype(bf16).reshape(adapters, rank_dim, hidden_cols)
+    return (jnp.concatenate(finished, axis=0), grad_a, grad_b)
+
+
 def solution(mesh):
+    small = mesh.shape["fsdp"] == 4 and mesh.shape["tensor"] == 4
     placed = (
         P(("group", "fsdp"), "tensor"),
         P(("group", "tensor"), "fsdp"),
@@ -88,7 +214,7 @@
         P("group"),
     )
     return jax.shard_map(
-        body,
+        body4 if small else body,
         mesh=mesh,
         in_specs=placed,
         out_specs=(

time: 366 us -> 226 us (0.62)
  waiting for transfers between devices: 255 us -> 24.8 us
  blocking collectives: 26.8 us -> 67.5 us
  starting transfers between devices: 0.38 us -> 38 us
  between operations: 13.9 us -> 1.29 us
  other arithmetic: 2.49 us -> 14.4 us
  local copies, waits for them, and re-layouts: 7.77 us -> 18 us
    reduce_scatter x2 -> x0, waiting for transfers between devices: 150 us -> none  [the longest x1 111 us: body(): lax.psum_scatter(lax.dot_general(gathered, base_weight, (((1,), (1,)), ((...]
    all_gather x2 -> x0, waiting for transfers between devices: 84.7 us -> none  [the longest x1 75.9 us: body(): gathered = lax.all_gather(grad_out, 'tensor', axis=0, tiled=True)]
    psum x1, blocking collectives: 12.3 us -> 67.5 us  [body4(): lax.psum(jnp.concatenate([grad_part, in_part], axis=1), ('tensor', 'fsdp'))]
    ppermute x0 -> x20, starting transfers between devices: none -> 38 us  [the longest x6 23.5 us: body4(): lax.ppermute(to_up.astype(bf16), 'fsdp', [(i, i + 1) for i in range(k)])]
    ppermute x0 -> x20, waiting for transfers between devices: none -> 24.8 us  [the longest x6 16.5 us: body4(): lax.ppermute(to_up.astype(bf16), 'fsdp', [(i, i + 1) for i in range(k)])]
    unnamed x6 -> x0, waiting for transfers between devices: 20.3 us -> none
    all_gather x1 -> x0, blocking collectives: 14.5 us -> none  [body(): lax.all_gather(low_in_b.reshape(host_rows, rank_dim), 'fsdp', axis=0, til...]
    convert_element_type x4 -> x13, other arithmetic: 2.49 us -> 9.87 us  [the longest x6 6.93 us: body4(): to_up.astype(bf16)]
  transfers between devices with their start and end apart: 5 -> 20, of which waited for: 5 -> 6; matrix products, arithmetic and copies ran while one was open for 15% -> 38% of each run, Pallas kernels for 0% -> 0%
where the time goes in v1:
time: 226 us; the launch traced here: 225 us
  blocking collectives  67.5 us (30%)
  matrix products  61.3 us (27%)
  starting transfers between devices  38 us (17%)
  waiting for transfers between devices  24.8 us (11%)
  local copies, waits for them, and re-layouts  18 us (8%)
  other arithmetic  14.4 us (6%)
    psum x1, blocking collectives, body4(): lax.psum(jnp.concatenate([grad_part, in_part], axis=1), ('tensor', 'fsdp'))  67.5 us
    dot_general x2, matrix products, body4(): lax.dot_general(gathered, base_weight, (((1,), (1,)), ((), ())), preferre...  37.2 us
    ppermute x6, starting transfers between devices, body4(): lax.ppermute(to_up.astype(bf16), 'fsdp', [(i, i + 1) for i in range(k)])  23.5 us
    ppermute x6, waiting for transfers between devices, body4(): lax.ppermute(to_up.astype(bf16), 'fsdp', [(i, i + 1) for i in range(k)])  16.5 us
    dot_general x2, matrix products, body4(): lax.dot_general(spread_in, gathered, (((0,), (0,)), ((), ())), preferred_...  15.4 us
    ppermute x8, starting transfers between devices, swap(): return lax.ppermute(value, axis, [(i, i ^ mask) for i in range(count)])  9.04 us
    convert_element_type x6, other arithmetic, body4(): to_up.astype(bf16)  6.93 us
    ppermute x6, starting transfers between devices, body4(): lax.ppermute(to_down.astype(bf16), 'fsdp', [(n - 1 - i, n - 2 - i) for i...  5.43 us
  transfers between devices with their start and end apart: 20, of which 6 were waited for; matrix products, arithmetic and copies ran while one was open for 38% of the time, Pallas kernels for 0%

profile of v1, /device:TPU:0, one launch (start us, length us, event | category | flops | bytes accessed | tf_op | source)
XLA Modules:
  0.0 225.3 jit_solution(11259563265881398934)
XLA Ops:
  0.7 2.3 %reshape.253 = bf16[192,4,512]{2,1,0:T(4,128)(2,1)S(1)} reshape(bf16[192,2048]{1,0:T(8,128)(2,1)} %param.7) | data formatting | bytes 1572864 | tf_op jit(solution)/shard_map/reshape | solution.py:115
  4.7 5.1 %collective-permute-start.5 = (bf16[192,512]{1,0:T(8,128)(2,1)S(1)}, bf16[192,512]{1,0:T(8,128)(2,1)S(1)}, u32[]{:S(2)}, u32[]{:S(2)}) collective-permute-start(bf16[192,512]{1,0:T(8,128)(2,1)S(1)} %bitcast.150), channel_id=1, source_target_pairs={{0,12},{4,8},{8,4},{12,0},{1,13},{5,9},{9,5},{13,1},{2,14},{6,10},... | collective-permute-start | bytes 589832 | tf_op jit(solution)/shard_map/ppermute | solution.py:83
  10.6 3.5 %fusion.53 = (bf16[96,7168]{1,0:T(8,128)(2,1)}, bf16[96,7168]{1,0:T(8,128)(2,1)}) fusion(bf16[192,7168]{1,0:T(8,128)(2,1)} %param.8), kind=kLoop, calls=%fused_computation.108 | loop fusion | bytes 5505024 | tf_op jit(solution)/shard_map/slice | solution.py:173
  16.6 5.0 %fusion.7 = f32[192,64]{0,1:T(8,128)S(1)} fusion(bf16[6,64,7168]{2,1,0:T(8,128)(2,1)} %param.11, bf16[192,7168]{1,0:T(8,128)(2,1)} %param.8, f32[192,6]{0,1:T(8,128)S(1)} %bitcast.153), kind=kOutput, calls=%fused_computation.13 | convolution fusion | flops 1057099776 | bytes 8311296 | tf_op jit(solution)/shard_map/dot_general | solution.py:143
  23.4 3.1 %collective-permute-done.4 = bf16[192,512]{1,0:T(8,128)(2,1)S(1)} collective-permute-done((bf16[192,512]{1,0:T(8,128)(2,1)S(1)}, bf16[192,512]{1,0:T(8,128)(2,1)S(1)}, u32[]{:S(2)}, u32[]{:S(2)}) %collective-permute-start.4) | collective-permute-done | bytes 196640 | tf_op jit(solution)/shard_map/ppermute | solution.py:83
  28.2 67.5 %all-reduce.1 = bf16[768,128]{0,1:T(8,128)(2,1)S(1)} all-reduce(f32[768,128]{0,1:T(8,128)S(1)} %pad_maximum_fusion.9), channel_id=1, replica_groups=mesh['group'=2,'fsdp'=4,'tensor'=4] {'tensor','fsdp'}, use_global_device_ids=true, to_apply=%region_2.3 | all-reduce | flops 98304 | bytes 589824 | tf_op jit(solution)/shard_map/psum | solution.py:151
  99.5 3.5 %fusion.52 = (bf16[96,7168]{1,0:T(8,128)(2,1)}, bf16[96,7168]{1,0:T(8,128)(2,1)}) fusion(bf16[192,7168]{1,0:T(8,128)(2,1)} %collective-permute-done), kind=kLoop, calls=%fused_computation.107 | loop fusion | bytes 5505024 | tf_op jit(solution)/shard_map/slice | solution.py:173
  104.0 18.7 %convolution_convert_fusion.1 = bf16[384,2048]{1,0:T(8,128)(2,1)} fusion(bf16[2048,7168]{1,0:T(8,128)(2,1)} %param.9, bf16[96,7168]{1,0:T(8,128)(2,1)} %copy-done.14, bf16[96,7168]{1,0:T(8,128)(2,1)} %collective-permute-done.1, bf16[96,7168]{1,0:T(8,128)(2,1)} %get-tuple-element.15, bf16[96,7168]{1,0:T(8,128)(2,1)} %get-tuple-element.17), kind=kOutput, calls=%fused_computation.4 | convolution fusion | flops 11297095680 | bytes 36438016 | tf_op jit(solution)/shard_map/dot_general | solution.py:174
  122.7 2.3 %fusion.24 = (bf16[96,2048]{1,0:T(8,128)(2,1)}, bf16[96,2048]{1,0:T(8,128)(2,1)}) fusion(bf16[4,96,2048]{2,1,0:T(8,128)(2,1)S(1)} %get-tuple-element.9, s32[]{:T(128)S(6)} %min.32, bf16[4,96,2048]{2,1,0:T(8,128)(2,1)} %bitcast.132, s32[]{:T(128)S(6)} %select_n.109, s32[]{:T(128)S(6)} %min.35, s32[]{:T(128)S(6)} %select_n.112), kind=kLoop, calls=%fused_computation.46 | loop fusion | flops 1572864 | bytes 2359312 | tf_op jit(solution)/shard_map/convert_element_type | solution.py:187
  125.0 2.0 collective-permute-start.6
  130.0 5.9 %collective-permute-done.6 = bf16[96,2048]{1,0:T(8,128)(2,1)} collective-permute-done((bf16[96,2048]{1,0:T(8,128)(2,1)}, bf16[96,2048]{1,0:T(8,128)(2,1)}, u32[]{:S(2)}, u32[]{:S(2)}) %collective-permute-start.6) | collective-permute-done | bytes 393248 | tf_op jit(solution)/shard_map/ppermute | solution.py:187
  137.1 4.4 %collective-permute-start.7 = (bf16[96,2048]{1,0:T(8,128)(2,1)S(1)}, bf16[96,2048]{1,0:T(8,128)(2,1)S(1)}, u32[]{:S(2)}, u32[]{:S(2)}) collective-permute-start(bf16[96,2048]{1,0:T(8,128)(2,1)S(1)} %fusion.20), channel_id=1, source_target_pairs={{0,4},{4,8},{1,5},{5,9},{2,6},{6,10},{3,7},{7,11},{16,20},{20,24},... | collective-permute-start | bytes 1179656 | tf_op jit(solution)/shard_map/ppermute | solution.py:187
  143.1 2.6 %convolution_bitcast_fusion = f32[6,512,64]{1,2,0:T(8,128)} fusion(bf16[768,512,1]{1,0,2:T(8,128)(2,1)} %bitcast.143, bf16[768,64]{0,1:T(8,128)(2,1)} %copy-done.10, bf16[768,6]{0,1:T(8,128)(2,1)} %copy-done.11), kind=kOutput, calls=%fused_computation.10 | convolution fusion | flops 302284800 | bytes 1680384 | tf_op jit(solution)/shard_map/dot_general | solution.py:156
  145.6 4.3 %collective-permute-done.7 = bf16[96,2048]{1,0:T(8,128)(2,1)S(1)} collective-permute-done((bf16[96,2048]{1,0:T(8,128)(2,1)S(1)}, bf16[96,2048]{1,0:T(8,128)(2,1)S(1)}, u32[]{:S(2)}, u32[]{:S(2)}) %collective-permute-start.7) | collective-permute-done | bytes 393248 | tf_op jit(solution)/shard_map/ppermute | solution.py:187
  151.9 5.8 %collective-permute-start.8 = (bf16[96,2048]{1,0:T(8,128)(2,1)}, bf16[96,2048]{1,0:T(8,128)(2,1)}, u32[]{:S(2)}, u32[]{:S(2)}) collective-permute-start(bf16[96,2048]{1,0:T(8,128)(2,1)} %get-tuple-element.5), channel_id=1, source_target_pairs={{0,4},{4,8},{8,12},{1,5},{5,9},{9,13},{2,6},{6,10},{10,14},{3,7},{... | collective-permute-start | bytes 1179656 | tf_op jit(solution)/shard_map/ppermute | solution.py:187
  157.7 18.6 %convolution_convert_fusion = bf16[384,2048]{1,0:T(8,128)(2,1)} fusion(bf16[2048,7168]{1,0:T(8,128)(2,1)} %param.9, bf16[96,7168]{1,0:T(8,128)(2,1)} %collective-permute-done.13, bf16[96,7168]{1,0:T(8,128)(2,1)} %collective-permute-done.12, bf16[96,7168]{1,0:T(8,128)(2,1)} %get-tuple-element.16, bf16[96,7168]{1,0:T(8,128)(2,1)} %get-tuple-element.4), kind=kOutput, calls=%fused_computation.3 | convolution fusion | flops 11297095680 | bytes 36438016 | tf_op jit(solution)/shard_map/dot_general | solution.py:174
  177.8 3.8 %collective-permute-start.14 = (bf16[96,2048]{1,0:T(8,128)(2,1)S(1)}, bf16[96,2048]{1,0:T(8,128)(2,1)S(1)}, u32[]{:S(2)}, u32[]{:S(2)}) collective-permute-start(bf16[96,2048]{1,0:T(8,128)(2,1)S(1)} %get-tuple-element.13), channel_id=1, source_target_pairs={{0,4},{1,5},{2,6},{3,7},{16,20},{17,21},{18,22},{19,23}} | collective-permute-start | bytes 1179656 | tf_op jit(solution)/shard_map/ppermute | solution.py:187
  184.8 3.8 %collective-permute-done.14 = bf16[96,2048]{1,0:T(8,128)(2,1)S(1)} collective-permute-done((bf16[96,2048]{1,0:T(8,128)(2,1)S(1)}, bf16[96,2048]{1,0:T(8,128)(2,1)S(1)}, u32[]{:S(2)}, u32[]{:S(2)}) %collective-permute-start.14) | collective-permute-done | bytes 393248 | tf_op jit(solution)/shard_map/ppermute | solution.py:187
  188.8 4.6 %collective-permute-start.15 = (bf16[96,2048]{1,0:T(8,128)(2,1)S(1)}, bf16[96,2048]{1,0:T(8,128)(2,1)S(1)}, u32[]{:S(2)}, u32[]{:S(2)}) collective-permute-start(bf16[96,2048]{1,0:T(8,128)(2,1)S(1)} %fusion.14), channel_id=1, source_target_pairs={{0,4},{4,8},{1,5},{5,9},{2,6},{6,10},{3,7},{7,11},{16,20},{20,24},... | collective-permute-start | bytes 1179656 | tf_op jit(solution)/shard_map/ppermute | solution.py:187
  193.5 7.3 %fusion.10 = f32[384,7168]{1,0:T(8,128)} fusion(bf16[384,384]{0,1:T(8,128)(2,1)S(1)} %bitcast.146, bf16[96,7168]{1,0:T(8,128)(2,1)} %collective-permute-done.13, bf16[96,7168]{1,0:T(8,128)(2,1)} %collective-permute-done.12, bf16[96,7168]{1,0:T(8,128)(2,1)S(1)} %copy-done.5, bf16[96,7168]{1,0:T(8,128)(2,1)} %get-tuple-element.4), kind=kOutput, calls=%fused_computation.14 | convolution fusion | flops 2135949312 | bytes 16809984 | tf_op jit(solution)/shard_map/dot_general | solution.py:197
  202.6 8.1 %add_convert_fusion = bf16[384,7168]{1,0:T(8,128)(2,1)} fusion(f32[384,7168]{1,0:T(8,128)} %fusion.10, bf16[384,384]{0,1:T(8,128)(2,1)S(1)} %bitcast.145, bf16[96,7168]{1,0:T(8,128)(2,1)S(1)} %copy-done.15, bf16[96,7168]{1,0:T(8,128)(2,1)} %collective-permute-done.1, bf16[96,7168]{1,0:T(8,128)(2,1)S(1)} %copy-done.4, bf16[96,7168]{1,0:T(8,128)(2,1)} %get-tuple-element.17), kind=kOutput, calls=%fused_computation | convolution fusion | flops 2141454336 | bytes 22315008 | tf_op jit(solution)/shard_map/dot_general | solution.py:197
  210.8 2.9 %collective-permute-start.16 = (bf16[96,2048]{1,0:T(8,128)(2,1)S(1)}, bf16[96,2048]{1,0:T(8,128)(2,1)S(1)}, u32[]{:S(2)}, u32[]{:S(2)}) collective-permute-start(bf16[96,2048]{1,0:T(8,128)(2,1)S(1)} %get-tuple-element.11), channel_id=1, source_target_pairs={{0,4},{4,8},{8,12},{1,5},{5,9},{9,13},{2,6},{6,10},{10,14},{3,7},{... | collective-permute-start | bytes 1179656 | tf_op jit(solution)/shard_map/ppermute | solution.py:187
  216.5 2.4 %collective-permute-done.16 = bf16[96,2048]{1,0:T(8,128)(2,1)S(1)} collective-permute-done((bf16[96,2048]{1,0:T(8,128)(2,1)S(1)}, bf16[96,2048]{1,0:T(8,128)(2,1)S(1)}, u32[]{:S(2)}, u32[]{:S(2)}) %collective-permute-start.16) | collective-permute-done | bytes 393248 | tf_op jit(solution)/shard_map/ppermute | solution.py:187
  218.9 5.2 %collective-permute-done.19 = bf16[96,2048]{1,0:T(8,128)(2,1)S(1)} collective-permute-done((bf16[96,2048]{1,0:T(8,128)(2,1)S(1)}, bf16[96,2048]{1,0:T(8,128)(2,1)S(1)}, u32[]{:S(2)}, u32[]{:S(2)}) %collective-permute-start.19) | collective-permute-done | bytes 393248 | tf_op jit(solution)/shard_map/ppermute | solution.py:188
  (117 shorter events, 31.3 us)
Async XLA Ops:
  0.6 27.0 %copy-start = (bf16[6,512,64]{1,2,0:T(8,128)(2,1)S(1)}, bf16[6,512,64]{1,2,0:T(8,128)(2,1)}, u32[]{:S(2)}) copy-start(bf16[6,512,64]{1,2,0:T(8,128)(2,1)} %param.10) | copy-start | bytes 1179652
  4.7 18.7 %collective-permute-start.5 = (bf16[192,512]{1,0:T(8,128)(2,1)S(1)}, bf16[192,512]{1,0:T(8,128)(2,1)S(1)}, u32[]{:S(2)}, u32[]{:S(2)}) collective-permute-start(bf16[192,512]{1,0:T(8,128)(2,1)S(1)} %bitcast.150), channel_id=1, source_target_pairs={{0,12},{4,8},{8,4},{12,0},{1,13},{5,9},{9,5},{13,1},{2,14},{6,10},... | collective-permute-start | bytes 589832 | tf_op jit(solution)/shard_map/ppermute | solution.py:83
  9.8 16.7 %collective-permute-start.4 = (bf16[192,512]{1,0:T(8,128)(2,1)S(1)}, bf16[192,512]{1,0:T(8,128)(2,1)S(1)}, u32[]{:S(2)}, u32[]{:S(2)}) collective-permute-start(bf16[192,512]{1,0:T(8,128)(2,1)S(1)} %bitcast.151), channel_id=1, source_target_pairs={{0,8},{4,12},{8,0},{12,4},{1,9},{5,13},{9,1},{13,5},{2,10},{6,14},... | collective-permute-start | bytes 589832 | tf_op jit(solution)/shard_map/ppermute | solution.py:83
  10.0 16.5 %collective-permute-start.3 = (bf16[192,512]{1,0:T(8,128)(2,1)S(1)}, bf16[192,512]{1,0:T(8,128)(2,1)S(1)}, u32[]{:S(2)}, u32[]{:S(2)}) collective-permute-start(bf16[192,512]{1,0:T(8,128)(2,1)S(1)} %bitcast.152), channel_id=1, source_target_pairs={{0,4},{4,0},{8,12},{12,8},{1,5},{5,1},{9,13},{13,9},{2,6},{6,2},{1... | collective-permute-start | bytes 589832 | tf_op jit(solution)/shard_map/ppermute | solution.py:83
  10.6 88.8 %collective-permute-start = (bf16[192,7168]{1,0:T(8,128)(2,1)}, bf16[192,7168]{1,0:T(8,128)(2,1)}, u32[]{:S(2)}, u32[]{:S(2)}) collective-permute-start(bf16[192,7168]{1,0:T(8,128)(2,1)} %param.8), channel_id=1, source_target_pairs={{0,1},{1,0},{2,3},{3,2},{4,5},{5,4},{6,7},{7,6},{8,9},{9,8},{10,11... | collective-permute-start | bytes 8257544 | tf_op jit(solution)/shard_map/ppermute | solution.py:83
  14.1 84.4 %collective-permute-start.1 = (bf16[96,7168]{1,0:T(8,128)(2,1)}, bf16[96,7168]{1,0:T(8,128)(2,1)}, u32[]{:S(2)}, u32[]{:S(2)}) collective-permute-start(bf16[96,7168]{1,0:T(8,128)(2,1)} %get-tuple-element.17), channel_id=1, source_target_pairs={{0,2},{1,3},{2,0},{3,1},{4,6},{5,7},{6,4},{7,5},{8,10},{9,11},{10,... | collective-permute-start | bytes 4128776 | tf_op jit(solution)/shard_map/ppermute | solution.py:83
  23.4 74.3 %copy-start.11 = (bf16[768,6]{0,1:T(8,128)(2,1)}, bf16[768,6]{0,1:T(8,128)(2,1)S(1)}, u32[]{:S(2)}) copy-start(bf16[768,6]{0,1:T(8,128)(2,1)S(1)} %fusion.46) | copy-start | bytes 27652
  98.5 30.9 %collective-permute-start.12 = (bf16[96,7168]{1,0:T(8,128)(2,1)}, bf16[96,7168]{1,0:T(8,128)(2,1)}, u32[]{:S(2)}, u32[]{:S(2)}) collective-permute-start(bf16[96,7168]{1,0:T(8,128)(2,1)} %get-tuple-element.4), channel_id=1, source_target_pairs={{0,2},{1,3},{2,0},{3,1},{4,6},{5,7},{6,4},{7,5},{8,10},{9,11},{10,... | collective-permute-start | bytes 4128776 | tf_op jit(solution)/shard_map/ppermute | solution.py:83
  99.5 3.5 %collective-permute-start.2 = (bf16[96,7168]{1,0:T(8,128)(2,1)}, bf16[96,7168]{1,0:T(8,128)(2,1)S(1)}, u32[]{:S(2)}, u32[]{:S(2)}) collective-permute-start(bf16[96,7168]{1,0:T(8,128)(2,1)} %collective-permute-done.1), channel_id=1, source_target_pairs={{0,1},{1,0},{2,3},{3,2},{4,5},{5,4},{6,7},{7,6},{8,9},{9,8},{10,11... | collective-permute-start | bytes 4128776 | tf_op jit(solution)/shard_map/ppermute | solution.py:83
  104.0 23.0 %copy-start.7 = (bf16[4,192,64]{1,0,2:T(4,128)(2,1)S(1)}, bf16[4,192,64]{1,0,2:T(4,128)(2,1)}, u32[]{:S(2)}) copy-start(bf16[4,192,64]{1,0,2:T(4,128)(2,1)} %maximum_convert_fusion) | copy-start | bytes 294916
  125.0 10.9 %collective-permute-start.6 = (bf16[96,2048]{1,0:T(8,128)(2,1)}, bf16[96,2048]{1,0:T(8,128)(2,1)}, u32[]{:S(2)}, u32[]{:S(2)}) collective-permute-start(bf16[96,2048]{1,0:T(8,128)(2,1)} %get-tuple-element.7), channel_id=1, source_target_pairs={{0,4},{1,5},{2,6},{3,7},{16,20},{17,21},{18,22},{19,23}} | collective-permute-start | bytes 1179656 | tf_op jit(solution)/shard_map/ppermute | solution.py:187
  127.9 22.0 %copy-start.2 = (bf16[384,2048]{1,0:T(8,128)(2,1)S(1)}, bf16[384,2048]{1,0:T(8,128)(2,1)}, u32[]{:S(2)}) copy-start(bf16[384,2048]{1,0:T(8,128)(2,1)} %convolution_convert_fusion.1) | copy-start | bytes 4718596
  128.7 16.9 %collective-permute-start.9 = (bf16[96,2048]{1,0:T(8,128)(2,1)}, bf16[96,2048]{1,0:T(8,128)(2,1)S(1)}, u32[]{:S(2)}, u32[]{:S(2)}) collective-permute-start(bf16[96,2048]{1,0:T(8,128)(2,1)} %get-tuple-element.8), channel_id=1, source_target_pairs={{12,8},{13,9},{14,10},{15,11},{28,24},{29,25},{30,26},{31,27}} | collective-permute-start | bytes 1179656 | tf_op jit(solution)/shard_map/ppermute | solution.py:188
  129.4 28.3 %collective-permute-start.13 = (bf16[96,7168]{1,0:T(8,128)(2,1)}, bf16[96,7168]{1,0:T(8,128)(2,1)}, u32[]{:S(2)}, u32[]{:S(2)}) collective-permute-start(bf16[96,7168]{1,0:T(8,128)(2,1)} %collective-permute-done.12), channel_id=1, source_target_pairs={{0,1},{1,0},{2,3},{3,2},{4,5},{5,4},{6,7},{7,6},{8,9},{9,8},{10,11... | collective-permute-start | bytes 4128776 | tf_op jit(solution)/shard_map/ppermute | solution.py:83
  137.1 12.8 %collective-permute-start.7 = (bf16[96,2048]{1,0:T(8,128)(2,1)S(1)}, bf16[96,2048]{1,0:T(8,128)(2,1)S(1)}, u32[]{:S(2)}, u32[]{:S(2)}) collective-permute-start(bf16[96,2048]{1,0:T(8,128)(2,1)S(1)} %fusion.20), channel_id=1, source_target_pairs={{0,4},{4,8},{1,5},{5,9},{2,6},{6,10},{3,7},{7,11},{16,20},{20,24},... | collective-permute-start | bytes 1179656 | tf_op jit(solution)/shard_map/ppermute | solution.py:187
  151.3 30.4 %collective-permute-start.10 = (bf16[96,2048]{1,0:T(8,128)(2,1)}, bf16[96,2048]{1,0:T(8,128)(2,1)S(1)}, u32[]{:S(2)}, u32[]{:S(2)}) collective-permute-start(bf16[96,2048]{1,0:T(8,128)(2,1)} %get-tuple-element.6), channel_id=1, source_target_pairs={{12,8},{8,4},{13,9},{9,5},{14,10},{10,6},{15,11},{11,7},{28,24},{2... | collective-permute-start | bytes 1179656 | tf_op jit(solution)/shard_map/ppermute | solution.py:188
  151.9 63.2 %collective-permute-start.8 = (bf16[96,2048]{1,0:T(8,128)(2,1)}, bf16[96,2048]{1,0:T(8,128)(2,1)}, u32[]{:S(2)}, u32[]{:S(2)}) collective-permute-start(bf16[96,2048]{1,0:T(8,128)(2,1)} %get-tuple-element.5), channel_id=1, source_target_pairs={{0,4},{4,8},{8,12},{1,5},{5,9},{9,13},{2,6},{6,10},{10,14},{3,7},{... | collective-permute-start | bytes 1179656 | tf_op jit(solution)/shard_map/ppermute | solution.py:187
  177.8 10.9 %collective-permute-start.14 = (bf16[96,2048]{1,0:T(8,128)(2,1)S(1)}, bf16[96,2048]{1,0:T(8,128)(2,1)S(1)}, u32[]{:S(2)}, u32[]{:S(2)}) collective-permute-start(bf16[96,2048]{1,0:T(8,128)(2,1)S(1)} %get-tuple-element.13), channel_id=1, source_target_pairs={{0,4},{1,5},{2,6},{3,7},{16,20},{17,21},{18,22},{19,23}} | collective-permute-start | bytes 1179656 | tf_op jit(solution)/shard_map/ppermute | solution.py:187
  182.9 32.3 %collective-permute-start.11 = (bf16[96,2048]{1,0:T(8,128)(2,1)S(1)}, bf16[96,2048]{1,0:T(8,128)(2,1)S(1)}, u32[]{:S(2)}, u32[]{:S(2)}) collective-permute-start(bf16[96,2048]{1,0:T(8,128)(2,1)S(1)} %fusion.19), channel_id=1, source_target_pairs={{12,8},{8,4},{4,0},{13,9},{9,5},{5,1},{14,10},{10,6},{6,2},{15,11}... | collective-permute-start | bytes 1179656 | tf_op jit(solution)/shard_map/ppermute | solution.py:188
  184.2 16.6 %collective-permute-start.17 = (bf16[96,2048]{1,0:T(8,128)(2,1)S(1)}, bf16[96,2048]{1,0:T(8,128)(2,1)S(1)}, u32[]{:S(2)}, u32[]{:S(2)}) collective-permute-start(bf16[96,2048]{1,0:T(8,128)(2,1)S(1)} %get-tuple-element.14), channel_id=1, source_target_pairs={{12,8},{13,9},{14,10},{15,11},{28,24},{29,25},{30,26},{31,27}} | collective-permute-start | bytes 1179656 | tf_op jit(solution)/shard_map/ppermute | solution.py:188
  188.8 12.0 %collective-permute-start.15 = (bf16[96,2048]{1,0:T(8,128)(2,1)S(1)}, bf16[96,2048]{1,0:T(8,128)(2,1)S(1)}, u32[]{:S(2)}, u32[]{:S(2)}) collective-permute-start(bf16[96,2048]{1,0:T(8,128)(2,1)S(1)} %fusion.14), channel_id=1, source_target_pairs={{0,4},{4,8},{1,5},{5,9},{2,6},{6,10},{3,7},{7,11},{16,20},{20,24},... | collective-permute-start | bytes 1179656 | tf_op jit(solution)/shard_map/ppermute | solution.py:187
  201.2 12.4 %collective-permute-start.18 = (bf16[96,2048]{1,0:T(8,128)(2,1)S(1)}, bf16[96,2048]{1,0:T(8,128)(2,1)S(1)}, u32[]{:S(2)}, u32[]{:S(2)}) collective-permute-start(bf16[96,2048]{1,0:T(8,128)(2,1)S(1)} %get-tuple-element.12), channel_id=1, source_target_pairs={{12,8},{8,4},{13,9},{9,5},{14,10},{10,6},{15,11},{11,7},{28,24},{2... | collective-permute-start | bytes 1179656 | tf_op jit(solution)/shard_map/ppermute | solution.py:188
  210.8 8.2 %collective-permute-start.16 = (bf16[96,2048]{1,0:T(8,128)(2,1)S(1)}, bf16[96,2048]{1,0:T(8,128)(2,1)S(1)}, u32[]{:S(2)}, u32[]{:S(2)}) collective-permute-start(bf16[96,2048]{1,0:T(8,128)(2,1)S(1)} %get-tuple-element.11), channel_id=1, source_target_pairs={{0,4},{4,8},{8,12},{1,5},{5,9},{9,13},{2,6},{6,10},{10,14},{3,7},{... | collective-permute-start | bytes 1179656 | tf_op jit(solution)/shard_map/ppermute | solution.py:187
  213.8 10.3 %collective-permute-start.19 = (bf16[96,2048]{1,0:T(8,128)(2,1)S(1)}, bf16[96,2048]{1,0:T(8,128)(2,1)S(1)}, u32[]{:S(2)}, u32[]{:S(2)}) collective-permute-start(bf16[96,2048]{1,0:T(8,128)(2,1)S(1)} %fusion.13), channel_id=1, source_target_pairs={{12,8},{8,4},{4,0},{13,9},{9,5},{5,1},{14,10},{10,6},{6,2},{15,11}... | collective-permute-start | bytes 1179656 | tf_op jit(solution)/shard_map/ppermute | solution.py:188
  (12 other events, 79.5 us)

commit v2 on v1

--- a/solution.py
+++ b/solution.py
@@ -139,18 +139,28 @@
 
     b_flat = factor_b.reshape(wide, hidden_cols)
     a_flat = jnp.transpose(factor_a, (1, 0, 2)).reshape(own_cols, wide)
+    def doubled(value):
+        value = value + swap(value, "fsdp", 1, n)
+        return value + swap(value, "fsdp", 2, n)
+
+    def every_block(value):
+        pair = jnp.stack([value, swap(value, "tensor", 1, n)])
+        return jnp.concatenate([pair, swap(pair, "tensor", 2, n)], axis=0)
+
+    own_member = take(member_blocks, t)
     grad_part = pick(
         lax.dot_general(grad_out, b_flat, (((1,), (1,)), ((), ())), preferred_element_type=f32),
-        take(member_blocks, t),
-    )
-    grad_part = lax.dynamic_update_index_in_dim(
-        jnp.zeros((n, host_rows, rank_dim), f32), grad_part, t, 0
-    ).reshape(total_rows, rank_dim)
+        own_member,
+    )
+    grad_order = every_block(doubled(grad_part).astype(bf16))
+    low_grad = ordered(grad_order, t).reshape(total_rows, rank_dim)
+
     rows_in = ordered(rows_in, z).reshape(total_rows, own_cols)
     in_part = pick(jnp.dot(rows_in, a_flat, preferred_element_type=f32), member)
-    low = lax.psum(jnp.concatenate([grad_part, in_part], axis=1), ("tensor", "fsdp"))
-    low_grad = low[:, :rank_dim]
-    low_in = low[:, rank_dim:]
+    by_core = in_part.reshape(2, 2, host_rows, rank_dim).transpose(1, 0, 2, 3)
+    halves = take(by_core, t % 2) + swap(take(by_core, 1 - t % 2), "tensor", 1, n)
+    own_in = take(halves, t // 2) + swap(take(halves, 1 - t // 2), "tensor", 2, n)
+    in_order = every_block(doubled(own_in).astype(bf16))
 
     spread_grad = spread(low_grad, member)
     grad_a = lax.dot_general(
@@ -163,7 +173,6 @@
         jnp.zeros((total_rows, feature_cols), bf16), low_rank.astype(bf16), z * own_cols, 1
     ).reshape(n, host_rows, feature_cols)
 
-    in_order = ordered(low_in.reshape(n, host_rows, rank_dim), t)
     member_order = ordered(member_blocks, t)
 
     grad_b = None

time: 226 us -> 216 us (0.956)
  blocking collectives: 67.5 us -> 0 us
  waiting for transfers between devices: 24.8 us -> 73.9 us
  starting transfers between devices: 38 us -> 46.7 us
    psum x1 -> x0, blocking collectives: 67.5 us -> none  [body4(): lax.psum(jnp.concatenate([grad_part, in_part], axis=1), ('tensor', 'fsdp'))]
    ppermute x8 -> x18, waiting for transfers between devices: 3.14 us -> 54.3 us  [swap(): return lax.ppermute(value, axis, [(i, i ^ mask) for i in range(count)])]
    ppermute x8 -> x18, starting transfers between devices: 9.04 us -> 17.1 us  [swap(): return lax.ppermute(value, axis, [(i, i ^ mask) for i in range(count)])]
  transfers between devices with their start and end apart: 20 -> 30, of which waited for: 6 -> 12; matrix products, arithmetic and copies ran while one was open for 38% -> 42% of each run, Pallas kernels for 0% -> 0%
where the time goes in v2:
time: 216 us; the launch traced here: 215 us
  waiting for transfers between devices  73.9 us (34%)
  matrix products  61.4 us (28%)
  starting transfers between devices  46.7 us (22%)
  local copies, waits for them, and re-layouts  17.5 us (8%)
  other arithmetic  14.5 us (7%)
    ppermute x18, waiting for transfers between devices, swap(): return lax.ppermute(value, axis, [(i, i ^ mask) for i in range(count)])  54.3 us
    dot_general x2, matrix products, body4(): lax.dot_general(gathered, base_weight, (((1,), (1,)), ((), ())), preferre...  37.3 us
    ppermute x6, starting transfers between devices, body4(): lax.ppermute(to_up.astype(bf16), 'fsdp', [(i, i + 1) for i in range(k)])  24 us
    ppermute x18, starting transfers between devices, swap(): return lax.ppermute(value, axis, [(i, i ^ mask) for i in range(count)])  17.1 us
    dot_general x2, matrix products, body4(): lax.dot_general(spread_in, gathered, (((0,), (0,)), ((), ())), preferred_...  15.4 us
    ppermute x6, waiting for transfers between devices, body4(): lax.ppermute(to_up.astype(bf16), 'fsdp', [(i, i + 1) for i in range(k)])  14.4 us
    convert_element_type x6, other arithmetic, body4(): to_up.astype(bf16)  6.97 us
    ppermute x6, starting transfers between devices, body4(): lax.ppermute(to_down.astype(bf16), 'fsdp', [(n - 1 - i, n - 2 - i) for i...  5.57 us
  transfers between devices with their start and end apart: 30, of which 12 were waited for; matrix products, arithmetic and copies ran while one was open for 42% of the time, Pallas kernels for 0%

profile of v2, /device:TPU:0, one launch (start us, length us, event | category | flops | bytes accessed | tf_op | source)
XLA Modules:
  0.0 215.3 jit_solution(8183365123730520533)
XLA Ops:
  3.0 5.1 %fusion.7 = f32[192,64]{0,1:T(8,128)S(1)} fusion(bf16[6,64,7168]{2,1,0:T(8,128)(2,1)} %param.11, bf16[192,7168]{1,0:T(8,128)(2,1)} %param.8, f32[192,6]{0,1:T(8,128)S(1)} %bitcast.175), kind=kOutput, calls=%fused_computation.13 | convolution fusion | flops 1057099776 | bytes 8311296 | tf_op jit(solution)/shard_map/dot_general | solution.py:152
  8.1 2.7 %collective-permute-start.3 = (f32[192,64]{0,1:T(8,128)S(1)}, f32[192,64]{0,1:T(8,128)S(1)}, u32[]{:S(2)}, u32[]{:S(2)}) collective-permute-start(f32[192,64]{0,1:T(8,128)S(1)} %fusion.7), channel_id=1, source_target_pairs={{0,4},{4,0},{8,12},{12,8},{1,5},{5,1},{9,13},{13,9},{2,6},{6,2},{1... | collective-permute-start | bytes 147464 | tf_op jit(solution)/shard_map/ppermute | solution.py:83
  13.1 2.5 %collective-permute-start.23 = (bf16[192,512]{1,0:T(8,128)(2,1)S(1)}, bf16[192,512]{1,0:T(8,128)(2,1)S(1)}, u32[]{:S(2)}, u32[]{:S(2)}) collective-permute-start(bf16[192,512]{1,0:T(8,128)(2,1)S(1)} %bitcast.167), channel_id=1, source_target_pairs={{0,12},{4,8},{8,4},{12,0},{1,13},{5,9},{9,5},{13,1},{2,14},{6,10},... | collective-permute-start | bytes 589832 | tf_op jit(solution)/shard_map/ppermute | solution.py:83
  17.7 3.5 %fusion.53 = (bf16[96,7168]{1,0:T(8,128)(2,1)}, bf16[96,7168]{1,0:T(8,128)(2,1)}) fusion(bf16[192,7168]{1,0:T(8,128)(2,1)} %param.8), kind=kLoop, calls=%fused_computation.120 | loop fusion | bytes 5505024 | tf_op jit(solution)/shard_map/slice | solution.py:182
  23.4 13.0 %collective-permute-done.4 = f32[192,64]{0,1:T(8,128)S(1)} collective-permute-done((f32[192,64]{0,1:T(8,128)S(1)}, f32[192,64]{0,1:T(8,128)S(1)}, u32[]{:S(2)}, u32[]{:S(2)}) %collective-permute-start.4) | collective-permute-done | bytes 49184 | tf_op jit(solution)/shard_map/ppermute | solution.py:83
  42.1 29.4 %collective-permute-done.6 = bf16[2,192,64]{1,2,0:T(8,128)(2,1)S(1)} collective-permute-done((bf16[2,192,64]{1,2,0:T(8,128)(2,1)S(1)}, bf16[2,192,64]{1,2,0:T(8,128)(2,1)S(1)}, u32[]{:S(2)}, u32[]{:S(2)}) %collective-permute-start.6) | collective-permute-done | bytes 49184 | tf_op jit(solution)/shard_map/ppermute | solution.py:83
  73.4 2.8 %collective-permute-done.25 = f32[192,64]{0,1:T(8,128)S(1)} collective-permute-done((f32[192,64]{0,1:T(8,128)S(1)}, f32[192,64]{0,1:T(8,128)S(1)}, u32[]{:S(2)}, u32[]{:S(2)}) %collective-permute-start.25) | collective-permute-done | bytes 49184 | tf_op jit(solution)/shard_map/ppermute | solution.py:83
  76.6 4.0 %collective-permute-done.26 = f32[192,64]{0,1:T(8,128)S(1)} collective-permute-done((f32[192,64]{0,1:T(8,128)S(1)}, f32[192,64]{0,1:T(8,128)S(1)}, u32[]{:S(2)}, u32[]{:S(2)}) %collective-permute-start.26) | collective-permute-done | bytes 49184 | tf_op jit(solution)/shard_map/ppermute | solution.py:83
  82.8 3.4 %collective-permute-done.27 = f32[192,64]{0,1:T(8,128)S(1)} collective-permute-done((f32[192,64]{0,1:T(8,128)S(1)}, f32[192,64]{0,1:T(8,128)S(1)}, u32[]{:S(2)}, u32[]{:S(2)}) %collective-permute-start.27) | collective-permute-done | bytes 49184 | tf_op jit(solution)/shard_map/ppermute | solution.py:83
  89.6 3.5 %fusion.52 = (bf16[96,7168]{1,0:T(8,128)(2,1)}, bf16[96,7168]{1,0:T(8,128)(2,1)}) fusion(bf16[192,7168]{1,0:T(8,128)(2,1)} %collective-permute-done), kind=kLoop, calls=%fused_computation.119 | loop fusion | bytes 5505024 | tf_op jit(solution)/shard_map/slice | solution.py:182
  94.1 18.7 %convolution_convert_fusion.1 = bf16[384,2048]{1,0:T(8,128)(2,1)} fusion(bf16[2048,7168]{1,0:T(8,128)(2,1)} %param.9, bf16[96,7168]{1,0:T(8,128)(2,1)} %copy-done.16, bf16[96,7168]{1,0:T(8,128)(2,1)} %collective-permute-done.1, bf16[96,7168]{1,0:T(8,128)(2,1)} %get-tuple-element.15, bf16[96,7168]{1,0:T(8,128)(2,1)} %get-tuple-element.17), kind=kOutput, calls=%fused_computation.4 | convolution fusion | flops 11297095680 | bytes 36438016 | tf_op jit(solution)/shard_map/dot_general | solution.py:183
  115.1 2.7 %collective-permute-start.7 = (bf16[96,2048]{1,0:T(8,128)(2,1)}, bf16[96,2048]{1,0:T(8,128)(2,1)}, u32[]{:S(2)}, u32[]{:S(2)}) collective-permute-start(bf16[96,2048]{1,0:T(8,128)(2,1)} %get-tuple-element.7), channel_id=1, source_target_pairs={{0,4},{1,5},{2,6},{3,7},{16,20},{17,21},{18,22},{19,23}} | collective-permute-start | bytes 1179656 | tf_op jit(solution)/shard_map/ppermute | solution.py:196
  123.2 3.3 %collective-permute-done.7 = bf16[96,2048]{1,0:T(8,128)(2,1)} collective-permute-done((bf16[96,2048]{1,0:T(8,128)(2,1)}, bf16[96,2048]{1,0:T(8,128)(2,1)}, u32[]{:S(2)}, u32[]{:S(2)}) %collective-permute-start.7) | collective-permute-done | bytes 393248 | tf_op jit(solution)/shard_map/ppermute | solution.py:196
  127.7 4.4 %collective-permute-start.8 = (bf16[96,2048]{1,0:T(8,128)(2,1)S(1)}, bf16[96,2048]{1,0:T(8,128)(2,1)S(1)}, u32[]{:S(2)}, u32[]{:S(2)}) collective-permute-start(bf16[96,2048]{1,0:T(8,128)(2,1)S(1)} %fusion.20), channel_id=1, source_target_pairs={{0,4},{4,8},{1,5},{5,9},{2,6},{6,10},{3,7},{7,11},{16,20},{20,24},... | collective-permute-start | bytes 1179656 | tf_op jit(solution)/shard_map/ppermute | solution.py:196
  135.3 5.1 %collective-permute-done.8 = bf16[96,2048]{1,0:T(8,128)(2,1)S(1)} collective-permute-done((bf16[96,2048]{1,0:T(8,128)(2,1)S(1)}, bf16[96,2048]{1,0:T(8,128)(2,1)S(1)}, u32[]{:S(2)}, u32[]{:S(2)}) %collective-permute-start.8) | collective-permute-done | bytes 393248 | tf_op jit(solution)/shard_map/ppermute | solution.py:196
  142.4 5.7 %collective-permute-start.9 = (bf16[96,2048]{1,0:T(8,128)(2,1)}, bf16[96,2048]{1,0:T(8,128)(2,1)}, u32[]{:S(2)}, u32[]{:S(2)}) collective-permute-start(bf16[96,2048]{1,0:T(8,128)(2,1)} %get-tuple-element.5), channel_id=1, source_target_pairs={{0,4},{4,8},{8,12},{1,5},{5,9},{9,13},{2,6},{6,10},{10,14},{3,7},{... | collective-permute-start | bytes 1179656 | tf_op jit(solution)/shard_map/ppermute | solution.py:196
  148.1 18.6 %convolution_convert_fusion = bf16[384,2048]{1,0:T(8,128)(2,1)} fusion(bf16[2048,7168]{1,0:T(8,128)(2,1)} %param.9, bf16[96,7168]{1,0:T(8,128)(2,1)} %collective-permute-done.14, bf16[96,7168]{1,0:T(8,128)(2,1)} %collective-permute-done.13, bf16[96,7168]{1,0:T(8,128)(2,1)} %get-tuple-element.16, bf16[96,7168]{1,0:T(8,128)(2,1)} %get-tuple-element.4), kind=kOutput, calls=%fused_computation.3 | convolution fusion | flops 11297095680 | bytes 36438016 | tf_op jit(solution)/shard_map/dot_general | solution.py:183
  168.2 3.9 %collective-permute-start.15 = (bf16[96,2048]{1,0:T(8,128)(2,1)S(1)}, bf16[96,2048]{1,0:T(8,128)(2,1)S(1)}, u32[]{:S(2)}, u32[]{:S(2)}) collective-permute-start(bf16[96,2048]{1,0:T(8,128)(2,1)S(1)} %get-tuple-element.13), channel_id=1, source_target_pairs={{0,4},{1,5},{2,6},{3,7},{16,20},{17,21},{18,22},{19,23}} | collective-permute-start | bytes 1179656 | tf_op jit(solution)/shard_map/ppermute | solution.py:196
  175.3 3.6 %collective-permute-done.15 = bf16[96,2048]{1,0:T(8,128)(2,1)S(1)} collective-permute-done((bf16[96,2048]{1,0:T(8,128)(2,1)S(1)}, bf16[96,2048]{1,0:T(8,128)(2,1)S(1)}, u32[]{:S(2)}, u32[]{:S(2)}) %collective-permute-start.15) | collective-permute-done | bytes 393248 | tf_op jit(solution)/shard_map/ppermute | solution.py:196
  179.0 4.4 %collective-permute-start.16 = (bf16[96,2048]{1,0:T(8,128)(2,1)S(1)}, bf16[96,2048]{1,0:T(8,128)(2,1)S(1)}, u32[]{:S(2)}, u32[]{:S(2)}) collective-permute-start(bf16[96,2048]{1,0:T(8,128)(2,1)S(1)} %fusion.14), channel_id=1, source_target_pairs={{0,4},{4,8},{1,5},{5,9},{2,6},{6,10},{3,7},{7,11},{16,20},{20,24},... | collective-permute-start | bytes 1179656 | tf_op jit(solution)/shard_map/ppermute | solution.py:196
  183.5 7.3 %fusion.10 = f32[384,7168]{1,0:T(8,128)} fusion(bf16[384,384]{0,1:T(8,128)(2,1)S(1)} %bitcast.158, bf16[96,7168]{1,0:T(8,128)(2,1)} %collective-permute-done.14, bf16[96,7168]{1,0:T(8,128)(2,1)} %collective-permute-done.13, bf16[96,7168]{1,0:T(8,128)(2,1)S(1)} %copy-done.5, bf16[96,7168]{1,0:T(8,128)(2,1)} %get-tuple-element.4), kind=kOutput, calls=%fused_computation.14 | convolution fusion | flops 2135949312 | bytes 16809984 | tf_op jit(solution)/shard_map/dot_general | solution.py:206
  192.6 8.1 %add_convert_fusion = bf16[384,7168]{1,0:T(8,128)(2,1)} fusion(f32[384,7168]{1,0:T(8,128)} %fusion.10, bf16[384,384]{0,1:T(8,128)(2,1)S(1)} %bitcast.157, bf16[96,7168]{1,0:T(8,128)(2,1)S(1)} %copy-done.17, bf16[96,7168]{1,0:T(8,128)(2,1)} %collective-permute-done.1, bf16[96,7168]{1,0:T(8,128)(2,1)S(1)} %copy-done.4, bf16[96,7168]{1,0:T(8,128)(2,1)} %get-tuple-element.17), kind=kOutput, calls=%fused_computation | convolution fusion | flops 2141454336 | bytes 22315008 | tf_op jit(solution)/shard_map/dot_general | solution.py:206
  200.7 2.9 %collective-permute-start.17 = (bf16[96,2048]{1,0:T(8,128)(2,1)S(1)}, bf16[96,2048]{1,0:T(8,128)(2,1)S(1)}, u32[]{:S(2)}, u32[]{:S(2)}) collective-permute-start(bf16[96,2048]{1,0:T(8,128)(2,1)S(1)} %get-tuple-element.11), channel_id=1, source_target_pairs={{0,4},{4,8},{8,12},{1,5},{5,9},{9,13},{2,6},{6,10},{10,14},{3,7},{... | collective-permute-start | bytes 1179656 | tf_op jit(solution)/shard_map/ppermute | solution.py:196
  208.9 5.2 %collective-permute-done.20 = bf16[96,2048]{1,0:T(8,128)(2,1)S(1)} collective-permute-done((bf16[96,2048]{1,0:T(8,128)(2,1)S(1)}, bf16[96,2048]{1,0:T(8,128)(2,1)S(1)}, u32[]{:S(2)}, u32[]{:S(2)}) %collective-permute-start.20) | collective-permute-done | bytes 393248 | tf_op jit(solution)/shard_map/ppermute | solution.py:197
  (152 shorter events, 50.3 us)
Async XLA Ops:
  0.6 88.9 %collective-permute-start = (bf16[192,7168]{1,0:T(8,128)(2,1)}, bf16[192,7168]{1,0:T(8,128)(2,1)}, u32[]{:S(2)}, u32[]{:S(2)}) collective-permute-start(bf16[192,7168]{1,0:T(8,128)(2,1)} %param.8), channel_id=1, source_target_pairs={{0,1},{1,0},{2,3},{3,2},{4,5},{5,4},{6,7},{7,6},{8,9},{9,8},{10,11... | collective-permute-start | bytes 8257544 | tf_op jit(solution)/shard_map/ppermute | solution.py:83
  8.1 13.5 %collective-permute-start.3 = (f32[192,64]{0,1:T(8,128)S(1)}, f32[192,64]{0,1:T(8,128)S(1)}, u32[]{:S(2)}, u32[]{:S(2)}) collective-permute-start(f32[192,64]{0,1:T(8,128)S(1)} %fusion.7), channel_id=1, source_target_pairs={{0,4},{4,0},{8,12},{12,8},{1,5},{5,1},{9,13},{13,9},{2,6},{6,2},{1... | collective-permute-start | bytes 147464 | tf_op jit(solution)/shard_map/ppermute | solution.py:83
  13.1 26.1 %collective-permute-start.23 = (bf16[192,512]{1,0:T(8,128)(2,1)S(1)}, bf16[192,512]{1,0:T(8,128)(2,1)S(1)}, u32[]{:S(2)}, u32[]{:S(2)}) collective-permute-start(bf16[192,512]{1,0:T(8,128)(2,1)S(1)} %bitcast.167), channel_id=1, source_target_pairs={{0,12},{4,8},{8,4},{12,0},{1,13},{5,9},{9,5},{13,1},{2,14},{6,10},... | collective-permute-start | bytes 589832 | tf_op jit(solution)/shard_map/ppermute | solution.py:83
  15.6 24.2 %collective-permute-start.22 = (bf16[192,512]{1,0:T(8,128)(2,1)S(1)}, bf16[192,512]{1,0:T(8,128)(2,1)S(1)}, u32[]{:S(2)}, u32[]{:S(2)}) collective-permute-start(bf16[192,512]{1,0:T(8,128)(2,1)S(1)} %bitcast.166), channel_id=1, source_target_pairs={{0,8},{4,12},{8,0},{12,4},{1,9},{5,13},{9,1},{13,5},{2,10},{6,14},... | collective-permute-start | bytes 589832 | tf_op jit(solution)/shard_map/ppermute | solution.py:83
  15.9 24.0 %collective-permute-start.21 = (bf16[192,512]{1,0:T(8,128)(2,1)S(1)}, bf16[192,512]{1,0:T(8,128)(2,1)S(1)}, u32[]{:S(2)}, u32[]{:S(2)}) collective-permute-start(bf16[192,512]{1,0:T(8,128)(2,1)S(1)} %bitcast.168), channel_id=1, source_target_pairs={{0,4},{4,0},{8,12},{12,8},{1,5},{5,1},{9,13},{13,9},{2,6},{6,2},{1... | collective-permute-start | bytes 589832 | tf_op jit(solution)/shard_map/ppermute | solution.py:83
  21.6 14.8 %collective-permute-start.4 = (f32[192,64]{0,1:T(8,128)S(1)}, f32[192,64]{0,1:T(8,128)S(1)}, u32[]{:S(2)}, u32[]{:S(2)}) collective-permute-start(f32[192,64]{0,1:T(8,128)S(1)} %add.289), channel_id=1, source_target_pairs={{0,8},{4,12},{8,0},{12,4},{1,9},{5,13},{9,1},{13,5},{2,10},{6,14},... | collective-permute-start | bytes 147464 | tf_op jit(solution)/shard_map/ppermute | solution.py:83
  37.7 51.3 %collective-permute-start.1 = (bf16[96,7168]{1,0:T(8,128)(2,1)}, bf16[96,7168]{1,0:T(8,128)(2,1)}, u32[]{:S(2)}, u32[]{:S(2)}) collective-permute-start(bf16[96,7168]{1,0:T(8,128)(2,1)} %get-tuple-element.17), channel_id=1, source_target_pairs={{0,2},{1,3},{2,0},{3,1},{4,6},{5,7},{6,4},{7,5},{8,10},{9,11},{10,... | collective-permute-start | bytes 4128776 | tf_op jit(solution)/shard_map/ppermute | solution.py:83
  39.2 32.3 %collective-permute-start.6 = (bf16[2,192,64]{1,2,0:T(8,128)(2,1)S(1)}, bf16[2,192,64]{1,2,0:T(8,128)(2,1)S(1)}, u32[]{:S(2)}, u32[]{:S(2)}) collective-permute-start(bf16[2,192,64]{1,2,0:T(8,128)(2,1)S(1)} %pad_maximum_fusion.12), channel_id=1, source_target_pairs={{0,2},{1,3},{2,0},{3,1},{4,6},{5,7},{6,4},{7,5},{8,10},{9,11},{10,... | collective-permute-start | bytes 147464 | tf_op jit(solution)/shard_map/ppermute | solution.py:83
  42.1 29.5 %collective-permute-start.24 = (f32[2,192,64]{1,0,2:T(2,128)S(1)}, f32[2,192,64]{1,0,2:T(2,128)S(1)}, u32[]{:S(2)}, u32[]{:S(2)}) collective-permute-start(f32[2,192,64]{1,0,2:T(2,128)S(1)} %bitcast.169), channel_id=1, source_target_pairs={{0,1},{1,0},{2,3},{3,2},{4,5},{5,4},{6,7},{7,6},{8,9},{9,8},{10,11... | collective-permute-start | bytes 294920 | tf_op jit(solution)/shard_map/ppermute | solution.py:83
  87.5 32.9 %collective-permute-start.29 = (bf16[2,192,64]{1,2,0:T(8,128)(2,1)S(1)}, bf16[2,192,64]{1,2,0:T(8,128)(2,1)S(1)}, u32[]{:S(2)}, u32[]{:S(2)}) collective-permute-start(bf16[2,192,64]{1,2,0:T(8,128)(2,1)S(1)} %pad_maximum_fusion.13), channel_id=1, source_target_pairs={{0,2},{1,3},{2,0},{3,1},{4,6},{5,7},{6,4},{7,5},{8,10},{9,11},{10,... | collective-permute-start | bytes 147464 | tf_op jit(solution)/shard_map/ppermute | solution.py:83
  89.0 33.9 %collective-permute-start.13 = (bf16[96,7168]{1,0:T(8,128)(2,1)}, bf16[96,7168]{1,0:T(8,128)(2,1)}, u32[]{:S(2)}, u32[]{:S(2)}) collective-permute-start(bf16[96,7168]{1,0:T(8,128)(2,1)} %get-tuple-element.4), channel_id=1, source_target_pairs={{0,2},{1,3},{2,0},{3,1},{4,6},{5,7},{6,4},{7,5},{8,10},{9,11},{10,... | collective-permute-start | bytes 4128776 | tf_op jit(solution)/shard_map/ppermute | solution.py:83
  115.1 11.3 %collective-permute-start.7 = (bf16[96,2048]{1,0:T(8,128)(2,1)}, bf16[96,2048]{1,0:T(8,128)(2,1)}, u32[]{:S(2)}, u32[]{:S(2)}) collective-permute-start(bf16[96,2048]{1,0:T(8,128)(2,1)} %get-tuple-element.7), channel_id=1, source_target_pairs={{0,4},{1,5},{2,6},{3,7},{16,20},{17,21},{18,22},{19,23}} | collective-permute-start | bytes 1179656 | tf_op jit(solution)/shard_map/ppermute | solution.py:196
  122.1 13.2 %collective-permute-start.10 = (bf16[96,2048]{1,0:T(8,128)(2,1)}, bf16[96,2048]{1,0:T(8,128)(2,1)S(1)}, u32[]{:S(2)}, u32[]{:S(2)}) collective-permute-start(bf16[96,2048]{1,0:T(8,128)(2,1)} %get-tuple-element.8), channel_id=1, source_target_pairs={{12,8},{13,9},{14,10},{15,11},{28,24},{29,25},{30,26},{31,27}} | collective-permute-start | bytes 1179656 | tf_op jit(solution)/shard_map/ppermute | solution.py:197
  122.9 25.2 %collective-permute-start.14 = (bf16[96,7168]{1,0:T(8,128)(2,1)}, bf16[96,7168]{1,0:T(8,128)(2,1)}, u32[]{:S(2)}, u32[]{:S(2)}) collective-permute-start(bf16[96,7168]{1,0:T(8,128)(2,1)} %collective-permute-done.13), channel_id=1, source_target_pairs={{0,1},{1,0},{2,3},{3,2},{4,5},{5,4},{6,7},{7,6},{8,9},{9,8},{10,11... | collective-permute-start | bytes 4128776 | tf_op jit(solution)/shard_map/ppermute | solution.py:83
  127.7 12.6 %collective-permute-start.8 = (bf16[96,2048]{1,0:T(8,128)(2,1)S(1)}, bf16[96,2048]{1,0:T(8,128)(2,1)S(1)}, u32[]{:S(2)}, u32[]{:S(2)}) collective-permute-start(bf16[96,2048]{1,0:T(8,128)(2,1)S(1)} %fusion.20), channel_id=1, source_target_pairs={{0,4},{4,8},{1,5},{5,9},{2,6},{6,10},{3,7},{7,11},{16,20},{20,24},... | collective-permute-start | bytes 1179656 | tf_op jit(solution)/shard_map/ppermute | solution.py:196
  141.7 30.4 %collective-permute-start.11 = (bf16[96,2048]{1,0:T(8,128)(2,1)}, bf16[96,2048]{1,0:T(8,128)(2,1)S(1)}, u32[]{:S(2)}, u32[]{:S(2)}) collective-permute-start(bf16[96,2048]{1,0:T(8,128)(2,1)} %get-tuple-element.6), channel_id=1, source_target_pairs={{12,8},{8,4},{13,9},{9,5},{14,10},{10,6},{15,11},{11,7},{28,24},{2... | collective-permute-start | bytes 1179656 | tf_op jit(solution)/shard_map/ppermute | solution.py:197
  142.4 62.7 %collective-permute-start.9 = (bf16[96,2048]{1,0:T(8,128)(2,1)}, bf16[96,2048]{1,0:T(8,128)(2,1)}, u32[]{:S(2)}, u32[]{:S(2)}) collective-permute-start(bf16[96,2048]{1,0:T(8,128)(2,1)} %get-tuple-element.5), channel_id=1, source_target_pairs={{0,4},{4,8},{8,12},{1,5},{5,9},{9,13},{2,6},{6,10},{10,14},{3,7},{... | collective-permute-start | bytes 1179656 | tf_op jit(solution)/shard_map/ppermute | solution.py:196
  168.2 10.6 %collective-permute-start.15 = (bf16[96,2048]{1,0:T(8,128)(2,1)S(1)}, bf16[96,2048]{1,0:T(8,128)(2,1)S(1)}, u32[]{:S(2)}, u32[]{:S(2)}) collective-permute-start(bf16[96,2048]{1,0:T(8,128)(2,1)S(1)} %get-tuple-element.13), channel_id=1, source_target_pairs={{0,4},{1,5},{2,6},{3,7},{16,20},{17,21},{18,22},{19,23}} | collective-permute-start | bytes 1179656 | tf_op jit(solution)/shard_map/ppermute | solution.py:196
  173.3 31.8 %collective-permute-start.12 = (bf16[96,2048]{1,0:T(8,128)(2,1)S(1)}, bf16[96,2048]{1,0:T(8,128)(2,1)S(1)}, u32[]{:S(2)}, u32[]{:S(2)}) collective-permute-start(bf16[96,2048]{1,0:T(8,128)(2,1)S(1)} %fusion.19), channel_id=1, source_target_pairs={{12,8},{8,4},{4,0},{13,9},{9,5},{5,1},{14,10},{10,6},{6,2},{15,11}... | collective-permute-start | bytes 1179656 | tf_op jit(solution)/shard_map/ppermute | solution.py:197
  174.6 16.2 %collective-permute-start.18 = (bf16[96,2048]{1,0:T(8,128)(2,1)S(1)}, bf16[96,2048]{1,0:T(8,128)(2,1)S(1)}, u32[]{:S(2)}, u32[]{:S(2)}) collective-permute-start(bf16[96,2048]{1,0:T(8,128)(2,1)S(1)} %get-tuple-element.14), channel_id=1, source_target_pairs={{12,8},{13,9},{14,10},{15,11},{28,24},{29,25},{30,26},{31,27}} | collective-permute-start | bytes 1179656 | tf_op jit(solution)/shard_map/ppermute | solution.py:197
  179.0 11.7 %collective-permute-start.16 = (bf16[96,2048]{1,0:T(8,128)(2,1)S(1)}, bf16[96,2048]{1,0:T(8,128)(2,1)S(1)}, u32[]{:S(2)}, u32[]{:S(2)}) collective-permute-start(bf16[96,2048]{1,0:T(8,128)(2,1)S(1)} %fusion.14), channel_id=1, source_target_pairs={{0,4},{4,8},{1,5},{5,9},{2,6},{6,10},{3,7},{7,11},{16,20},{20,24},... | collective-permute-start | bytes 1179656 | tf_op jit(solution)/shard_map/ppermute | solution.py:196
  191.2 12.4 %collective-permute-start.19 = (bf16[96,2048]{1,0:T(8,128)(2,1)S(1)}, bf16[96,2048]{1,0:T(8,128)(2,1)S(1)}, u32[]{:S(2)}, u32[]{:S(2)}) collective-permute-start(bf16[96,2048]{1,0:T(8,128)(2,1)S(1)} %get-tuple-element.12), channel_id=1, source_target_pairs={{12,8},{8,4},{13,9},{9,5},{14,10},{10,6},{15,11},{11,7},{28,24},{2... | collective-permute-start | bytes 1179656 | tf_op jit(solution)/shard_map/ppermute | solution.py:197
  200.7 8.1 %collective-permute-start.17 = (bf16[96,2048]{1,0:T(8,128)(2,1)S(1)}, bf16[96,2048]{1,0:T(8,128)(2,1)S(1)}, u32[]{:S(2)}, u32[]{:S(2)}) collective-permute-start(bf16[96,2048]{1,0:T(8,128)(2,1)S(1)} %get-tuple-element.11), channel_id=1, source_target_pairs={{0,4},{4,8},{8,12},{1,5},{5,9},{9,13},{2,6},{6,10},{10,14},{3,7},{... | collective-permute-start | bytes 1179656 | tf_op jit(solution)/shard_map/ppermute | solution.py:196
  203.8 10.3 %collective-permute-start.20 = (bf16[96,2048]{1,0:T(8,128)(2,1)S(1)}, bf16[96,2048]{1,0:T(8,128)(2,1)S(1)}, u32[]{:S(2)}, u32[]{:S(2)}) collective-permute-start(bf16[96,2048]{1,0:T(8,128)(2,1)S(1)} %fusion.13), channel_id=1, source_target_pairs={{12,8},{8,4},{4,0},{13,9},{9,5},{5,1},{14,10},{10,6},{6,2},{15,11}... | collective-permute-start | bytes 1179656 | tf_op jit(solution)/shard_map/ppermute | solution.py:197
  (24 other events, 272.2 us)

commit v3 on v2

--- a/solution.py
+++ b/solution.py
@@ -102,15 +102,15 @@
     bf16, f32 = jnp.bfloat16, jnp.float32
 
     mate = swap(grad_out, "tensor", 1, n)
-    pieces = []
-    across = None
-    for c in range(chunks):
-        sent = grad_out[c * step_rows : (c + 1) * step_rows]
-        if across is not None:
-            sent = after(sent, across)
-        across = swap(sent, "tensor", 2, n)
-        relayed = swap(across, "tensor", 1, n)
-        pieces.append((c, across, relayed))
+    legs = 2 * chunks
+    leg_rows = host_rows // legs
+    across, relayed = [], []
+    for c in range(legs):
+        sent = grad_out[c * leg_rows : (c + 1) * leg_rows]
+        if across:
+            sent = after(sent, across[-1])
+        across.append(swap(sent, "tensor", 2, n))
+        relayed.append(swap(across[-1], "tensor", 1, n))
 
     by_owner = inputs.reshape(host_rows, n, own_cols).transpose(1, 0, 2)
     kept = take(by_owner, z)
@@ -143,8 +143,9 @@
         value = value + swap(value, "fsdp", 1, n)
         return value + swap(value, "fsdp", 2, n)
 
-    def every_block(value):
+    def every_block(value, leg):
         pair = jnp.stack([value, swap(value, "tensor", 1, n)])
+        pair = after(pair, across[leg])
         return jnp.concatenate([pair, swap(pair, "tensor", 2, n)], axis=0)
 
     own_member = take(member_blocks, t)
@@ -152,15 +153,16 @@
         lax.dot_general(grad_out, b_flat, (((1,), (1,)), ((), ())), preferred_element_type=f32),
         own_member,
     )
-    grad_order = every_block(doubled(grad_part).astype(bf16))
+    grad_order = every_block(doubled(grad_part).astype(bf16), 0)
     low_grad = ordered(grad_order, t).reshape(total_rows, rank_dim)
 
     rows_in = ordered(rows_in, z).reshape(total_rows, own_cols)
     in_part = pick(jnp.dot(rows_in, a_flat, preferred_element_type=f32), member)
     by_core = in_part.reshape(2, 2, host_rows, rank_dim).transpose(1, 0, 2, 3)
     halves = take(by_core, t % 2) + swap(take(by_core, 1 - t % 2), "tensor", 1, n)
-    own_in = take(halves, t // 2) + swap(take(halves, 1 - t // 2), "tensor", 2, n)
-    in_order = every_block(doubled(own_in).astype(bf16))
+    other = after(take(halves, 1 - t // 2), across[1])
+    own_in = take(halves, t // 2) + swap(other, "tensor", 2, n)
+    in_order = every_block(doubled(own_in).astype(bf16), 2)
 
     spread_grad = spread(low_grad, member)
     grad_a = lax.dot_general(
@@ -176,10 +178,15 @@
     member_order = ordered(member_blocks, t)
 
     grad_b = None
-    finished = []
-    for c, across, relayed in pieces:
+    finished, passed, operands = [], [], []
+    for c in range(chunks):
         rows = slice(c * step_rows, (c + 1) * step_rows)
-        gathered = jnp.concatenate([grad_out[rows], mate[rows], across, relayed], axis=0)
+        here = slice(2 * c, 2 * c + 2)
+        gathered = jnp.concatenate(
+            [grad_out[rows], mate[rows]] + across[here] + relayed[here], axis=0
+        )
+        if passed:
+            gathered = after(gathered, passed[n - 3])
         part = lax.dot_general(
             gathered, base_weight, (((1,), (1,)), ((), ())), preferred_element_type=f32
         ).astype(bf16).reshape(n, step_rows, feature_cols)
@@ -188,7 +195,13 @@
             dest = jnp.clip(dest, 0, n - 1)
             return take(part, dest ^ t).astype(f32) + take(low_rank[:, rows], dest).astype(f32)
 
+        spread_in = spread(
+            in_order[:, rows].reshape(n * step_rows, rank_dim),
+            member_order[:, rows].reshape(n * step_rows, adapters),
+        )
+        operands.append((spread_in, gathered))
         up = down = None
+        passed = []
         for k in range(1, n):
             to_up, to_down = own(z + n - k), own(z - n + k)
             if up is not None:
@@ -197,16 +210,20 @@
             down = lax.ppermute(
                 to_down.astype(bf16), "fsdp", [(n - 1 - i, n - 2 - i) for i in range(k)]
             )
+            if c == chunks - 1 and k > 1:
+                spread_in, gathered = operands[k - 2]
+                term = lax.dot_general(
+                    after(spread_in, passed[-1]),
+                    gathered,
+                    (((0,), (0,)), ((), ())),
+                    preferred_element_type=f32,
+                )
+                grad_b = term if grad_b is None else grad_b + term
+                if k < n - 1:
+                    grad_b, up, down = lax.optimization_barrier((grad_b, up, down))
+            passed.append((up, down))
         finished.append((own(z) + up.astype(f32) + down.astype(f32)).astype(bf16))
 
-        spread_in = spread(
-            in_order[:, rows].reshape(n * step_rows, rank_dim),
-            member_order[:, rows].reshape(n * step_rows, adapters),
-        )
-        term = lax.dot_general(
-            spread_in, gathered, (((0,), (0,)), ((), ())), preferred_element_type=f32
-        )
-        grad_b = term if grad_b is None else grad_b + term
     grad_b = grad_b.astype(bf16).reshape(adapters, rank_dim, hidden_cols)
     return (jnp.concatenate(finished, axis=0), grad_a, grad_b)
 

time: 216 us -> 226 us (1.046)
  starting transfers between devices: 46.7 us -> 65.3 us
  local copies, waits for them, and re-layouts: 17.5 us -> 32.2 us
  waiting for transfers between devices: 73.9 us -> 62.1 us
  matrix products: 61.4 us -> 51.6 us
    unnamed x43 -> x39, local copies, waits for them, and re-layouts: 2.79 us -> 18.1 us
    ppermute x6, starting transfers between devices: 24 us -> 37.9 us  [body4(): lax.ppermute(to_up.astype(bf16), 'fsdp', [(i, i + 1) for i in range(k)])]
    dot_general x2, matrix products: 15.4 us -> 7.99 us  [body4(): lax.dot_general(after(spread_in, passed[-1]), gathered, (((0,), (0,)), ((...]
    ppermute x18 -> x22, waiting for transfers between devices: 54.3 us -> 48.6 us  [swap(): return lax.ppermute(value, axis, [(i, i ^ mask) for i in range(count)])]
    convert_element_type x6 -> x3, other arithmetic: 6.97 us -> 1.7 us  [body4(): to_up.astype(bf16)]
    ppermute x6, waiting for transfers between devices: 5.22 us -> 0.02 us  [body4(): lax.ppermute(to_down.astype(bf16), 'fsdp', [(n - 1 - i, n - 2 - i) for i...]
    ppermute x18 -> x22, starting transfers between devices: 17.1 us -> 21.2 us  [swap(): return lax.ppermute(value, axis, [(i, i ^ mask) for i in range(count)])]
    slice x2 -> x1, local copies, waits for them, and re-layouts: 6.94 us -> 3.08 us  [body4(): sent = grad_out[c * leg_rows:(c + 1) * leg_rows]]
  transfers between devices with their start and end apart: 30 -> 34, of which waited for: 12 -> 12; matrix products, arithmetic and copies ran while one was open for 42% -> 40% of each run, Pallas kernels for 0% -> 0%
where the time goes in v3:
time: 226 us; the launch traced here: 225 us
  starting transfers between devices  65.3 us (29%)
  waiting for transfers between devices  62.1 us (27%)
  matrix products  51.6 us (23%)
  local copies, waits for them, and re-layouts  32.2 us (14%)
  other arithmetic  12.6 us (6%)
    ppermute x22, waiting for transfers between devices, swap(): return lax.ppermute(value, axis, [(i, i ^ mask) for i in range(count)])  48.6 us
    ppermute x6, starting transfers between devices, body4(): lax.ppermute(to_up.astype(bf16), 'fsdp', [(i, i + 1) for i in range(k)])  37.9 us
    dot_general x2, matrix products, body4(): lax.dot_general(gathered, base_weight, (((1,), (1,)), ((), ())), preferre...  36.1 us
    ppermute x22, starting transfers between devices, swap(): return lax.ppermute(value, axis, [(i, i ^ mask) for i in range(count)])  21.2 us
    unnamed x39, local copies, waits for them, and re-layouts  18.1 us
    ppermute x6, waiting for transfers between devices, body4(): lax.ppermute(to_up.astype(bf16), 'fsdp', [(i, i + 1) for i in range(k)])  13.5 us
    dot_general x2, matrix products, body4(): lax.dot_general(after(spread_in, passed[-1]), gathered, (((0,), (0,)), ((...  7.99 us
    ppermute x6, starting transfers between devices, body4(): lax.ppermute(to_down.astype(bf16), 'fsdp', [(n - 1 - i, n - 2 - i) for i...  6.21 us
  transfers between devices with their start and end apart: 34, of which 12 were waited for; matrix products, arithmetic and copies ran while one was open for 40% of the time, Pallas kernels for 0%

profile of v3, /device:TPU:0, one launch (start us, length us, event | category | flops | bytes accessed | tf_op | source)
XLA Modules:
  0.0 225.3 jit_solution(526266138287896281)
XLA Ops:
  4.7 5.1 %collective-permute-start.21 = (bf16[192,512]{1,0:T(8,128)(2,1)S(1)}, bf16[192,512]{1,0:T(8,128)(2,1)S(1)}, u32[]{:S(2)}, u32[]{:S(2)}) collective-permute-start(bf16[192,512]{1,0:T(8,128)(2,1)S(1)} %bitcast.169), channel_id=1, source_target_pairs={{0,12},{4,8},{8,4},{12,0},{1,13},{5,9},{9,5},{13,1},{2,14},{6,10},... | collective-permute-start | bytes 589832 | tf_op jit(solution)/shard_map/ppermute | solution.py:83
  11.2 5.0 %fusion.7 = f32[192,64]{0,1:T(8,128)S(1)} fusion(bf16[6,64,7168]{2,1,0:T(8,128)(2,1)} %param.11, bf16[192,7168]{1,0:T(8,128)(2,1)} %param.8, f32[192,6]{0,1:T(8,128)S(1)} %bitcast.177), kind=kOutput, calls=%fused_computation.15 | convolution fusion | flops 1057099776 | bytes 8311296 | tf_op jit(solution)/shard_map/dot_general | solution.py:153
  17.7 3.1 %fusion.47 = (bf16[48,7168]{1,0:T(8,128)(2,1)}, bf16[48,7168]{1,0:T(8,128)(2,1)S(1)}, bf16[48,7168]{1,0:T(8,128)(2,1)}, bf16[48,7168]{1,0:T(8,128)(2,1)}) fusion(bf16[192,7168]{1,0:T(8,128)(2,1)} %param.8), kind=kLoop, calls=%fused_computation.126 | loop fusion | bytes 5505024 | tf_op jit(solution)/shard_map/slice | solution.py:109
  21.1 3.5 %slice_dynamic-update-slice_fusion.3 = (bf16[384,7168]{1,0:T(8,128)(2,1)}, bf16[384,7168]{1,0:T(8,128)(2,1)}) fusion(bf16[192,7168]{1,0:T(8,128)(2,1)} %param.8), kind=kLoop, calls=%fused_computation.11 | loop fusion | bytes 5505024
  28.0 3.3 %collective-permute-done.6 = f32[192,64]{0,1:T(8,128)S(1)} collective-permute-done((f32[192,64]{0,1:T(8,128)S(1)}, f32[192,64]{0,1:T(8,128)S(1)}, u32[]{:S(2)}, u32[]{:S(2)}) %collective-permute-start.6) | collective-permute-done | bytes 49184 | tf_op jit(solution)/shard_map/ppermute | solution.py:83
  35.1 14.0 %collective-permute-done.1 = bf16[48,7168]{1,0:T(8,128)(2,1)} collective-permute-done((bf16[48,7168]{1,0:T(8,128)(2,1)}, bf16[48,7168]{1,0:T(8,128)(2,1)}, u32[]{:S(2)}, u32[]{:S(2)}) %collective-permute-start.1) | collective-permute-done | bytes 688160 | tf_op jit(solution)/shard_map/ppermute | solution.py:83
  51.4 15.6 %collective-permute-done.8 = bf16[2,192,64]{1,2,0:T(8,128)(2,1)S(1)} collective-permute-done((bf16[2,192,64]{1,2,0:T(8,128)(2,1)S(1)}, bf16[2,192,64]{1,2,0:T(8,128)(2,1)S(1)}, u32[]{:S(2)}, u32[]{:S(2)}) %collective-permute-start.8) | collective-permute-done | bytes 49184 | tf_op jit(solution)/shard_map/ppermute | solution.py:83
  77.9 3.7 %collective-permute-done.25 = f32[192,64]{0,1:T(8,128)S(1)} collective-permute-done((f32[192,64]{0,1:T(8,128)S(1)}, f32[192,64]{0,1:T(8,128)S(1)}, u32[]{:S(2)}, u32[]{:S(2)}) %collective-permute-start.25) | collective-permute-done | bytes 49184 | tf_op jit(solution)/shard_map/ppermute | solution.py:83
  83.6 4.5 %collective-permute-done.15 = bf16[48,7168]{1,0:T(8,128)(2,1)} collective-permute-done((bf16[48,7168]{1,0:T(8,128)(2,1)}, bf16[48,7168]{1,0:T(8,128)(2,1)}, u32[]{:S(2)}, u32[]{:S(2)}) %collective-permute-start.15) | collective-permute-done | bytes 688160 | tf_op jit(solution)/shard_map/ppermute | solution.py:83
  93.7 3.5 %slice_dynamic-update-slice_fusion.1 = (bf16[384,7168]{1,0:T(8,128)(2,1)}, bf16[384,7168]{1,0:T(8,128)(2,1)}) fusion(bf16[384,7168]{1,0:T(8,128)(2,1)} %get-tuple-element.41, bf16[192,7168]{1,0:T(8,128)(2,1)} %collective-permute-done, bf16[384,7168]{1,0:T(8,128)(2,1)} %get-tuple-element.42), kind=kLoop, calls=%fused_computation.9 | loop fusion | bytes 5505024
  104.1 17.6 %convolution_convert_fusion.1 = bf16[384,2048]{1,0:T(8,128)(2,1)S(1)} fusion(bf16[384,7168]{1,0:T(8,128)(2,1)} %constant_dynamic-update-slice_fusion, bf16[2048,7168]{1,0:T(8,128)(2,1)} %param.9), kind=kOutput, calls=%fused_computation.2 | convolution fusion | flops 11275075584 | bytes 36438016 | tf_op jit(solution)/shard_map/dot_general | solution.py:190
  121.9 4.0 %collective-permute-start.9 = (bf16[96,2048]{1,0:T(8,128)(2,1)S(1)}, bf16[96,2048]{1,0:T(8,128)(2,1)S(1)}, u32[]{:S(2)}, u32[]{:S(2)}) collective-permute-start(bf16[96,2048]{1,0:T(8,128)(2,1)S(1)} %get-tuple-element.36), channel_id=1, source_target_pairs={{0,4},{1,5},{2,6},{3,7},{16,20},{17,21},{18,22},{19,23}} | collective-permute-start | bytes 1179656 | tf_op jit(solution)/shard_map/ppermute | solution.py:209
  130.8 4.1 %collective-permute-done.9 = bf16[96,2048]{1,0:T(8,128)(2,1)S(1)} collective-permute-done((bf16[96,2048]{1,0:T(8,128)(2,1)S(1)}, bf16[96,2048]{1,0:T(8,128)(2,1)S(1)}, u32[]{:S(2)}, u32[]{:S(2)}) %collective-permute-start.9) | collective-permute-done | bytes 393248 | tf_op jit(solution)/shard_map/ppermute | solution.py:209
  135.0 4.4 %collective-permute-start.10 = (bf16[96,2048]{1,0:T(8,128)(2,1)S(1)}, bf16[96,2048]{1,0:T(8,128)(2,1)S(1)}, u32[]{:S(2)}, u32[]{:S(2)}) collective-permute-start(bf16[96,2048]{1,0:T(8,128)(2,1)S(1)} %fusion.19), channel_id=1, source_target_pairs={{0,4},{4,8},{1,5},{5,9},{2,6},{6,10},{3,7},{7,11},{16,20},{20,24},... | collective-permute-start | bytes 1179656 | tf_op jit(solution)/shard_map/ppermute | solution.py:209
  141.5 6.2 %collective-permute-done.10 = bf16[96,2048]{1,0:T(8,128)(2,1)S(1)} collective-permute-done((bf16[96,2048]{1,0:T(8,128)(2,1)S(1)}, bf16[96,2048]{1,0:T(8,128)(2,1)S(1)}, u32[]{:S(2)}, u32[]{:S(2)}) %collective-permute-start.10) | collective-permute-done | bytes 393248 | tf_op jit(solution)/shard_map/ppermute | solution.py:209
  151.2 4.5 %collective-permute-start.11 = (bf16[96,2048]{1,0:T(8,128)(2,1)}, bf16[96,2048]{1,0:T(8,128)(2,1)S(1)}, u32[]{:S(2)}, u32[]{:S(2)}) collective-permute-start(bf16[96,2048]{1,0:T(8,128)(2,1)} %get-tuple-element.27), channel_id=1, source_target_pairs={{0,4},{4,8},{8,12},{1,5},{5,9},{9,13},{2,6},{6,10},{10,14},{3,7},{... | collective-permute-start | bytes 1179656 | tf_op jit(solution)/shard_map/ppermute | solution.py:209
  155.7 18.5 %convolution_convert_fusion = bf16[384,2048]{1,0:T(8,128)(2,1)} fusion(bf16[384,7168]{1,0:T(8,128)(2,1)} %constant_dynamic-update-slice_fusion.6, bf16[2048,7168]{1,0:T(8,128)(2,1)} %param.9), kind=kOutput, calls=%fused_computation.1 | convolution fusion | flops 11275075584 | bytes 36438016 | tf_op jit(solution)/shard_map/dot_general | solution.py:190
  175.6 9.4 %collective-permute-start.28 = (bf16[96,2048]{1,0:T(8,128)(2,1)S(1)}, bf16[96,2048]{1,0:T(8,128)(2,1)S(1)}, u32[]{:S(2)}, u32[]{:S(2)}) collective-permute-start(bf16[96,2048]{1,0:T(8,128)(2,1)S(1)} %get-tuple-element.34), channel_id=1, source_target_pairs={{0,4},{1,5},{2,6},{3,7},{16,20},{17,21},{18,22},{19,23}} | collective-permute-start | bytes 1179656 | tf_op jit(solution)/shard_map/ppermute | solution.py:209
  188.4 3.0 %collective-permute-done.28 = bf16[96,2048]{1,0:T(8,128)(2,1)S(1)} collective-permute-done((bf16[96,2048]{1,0:T(8,128)(2,1)S(1)}, bf16[96,2048]{1,0:T(8,128)(2,1)S(1)}, u32[]{:S(2)}, u32[]{:S(2)}) %collective-permute-start.28) | collective-permute-done | bytes 393248 | tf_op jit(solution)/shard_map/ppermute | solution.py:209
  192.9 4.4 %collective-permute-start.30 = (bf16[96,2048]{1,0:T(8,128)(2,1)S(1)}, bf16[96,2048]{1,0:T(8,128)(2,1)S(1)}, u32[]{:S(2)}, u32[]{:S(2)}) collective-permute-start(bf16[96,2048]{1,0:T(8,128)(2,1)S(1)} %get-tuple-element.32), channel_id=1, source_target_pairs={{0,4},{4,8},{1,5},{5,9},{2,6},{6,10},{3,7},{7,11},{16,20},{20,24},... | collective-permute-start | bytes 1179656 | tf_op jit(solution)/shard_map/ppermute | solution.py:209
  198.2 3.0 %fusion.50 = f32[384,7168]{1,0:T(8,128)S(1)} fusion(bf16[384,384]{0,1:T(8,128)(2,1)S(1)} %bitcast.161, bf16[384,7168]{1,0:T(8,128)(2,1)S(1)} %bitcast.148), kind=kOutput, calls=%fused_computation.129 | convolution fusion | flops 2113929216 | bytes 16809984 | tf_op jit(solution)/shard_map/dot_general | solution.py:215
  204.5 11.3 %collective-permute-start.32 = (bf16[96,2048]{1,0:T(8,128)(2,1)S(1)}, bf16[96,2048]{1,0:T(8,128)(2,1)S(1)}, u32[]{:S(2)}, u32[]{:S(2)}) collective-permute-start(bf16[96,2048]{1,0:T(8,128)(2,1)S(1)} %get-tuple-element.29), channel_id=1, source_target_pairs={{0,4},{4,8},{8,12},{1,5},{5,9},{9,13},{2,6},{6,10},{10,14},{3,7},{... | collective-permute-start | bytes 1179656 | tf_op jit(solution)/shard_map/ppermute | solution.py:209
  215.8 5.0 %fusion.51 = f32[384,7168]{1,0:T(8,128)S(1)} fusion(bf16[384,384]{0,1:T(8,128)(2,1)S(1)} %bitcast.160, bf16[384,7168]{1,0:T(8,128)(2,1)} %constant_dynamic-update-slice_fusion.6), kind=kOutput, calls=%fused_computation.130 | convolution fusion | flops 2113929216 | bytes 16809984 | tf_op jit(solution)/shard_map/dot_general | solution.py:215
  220.8 3.2 %add_convert_fusion = bf16[384,7168]{1,0:T(8,128)(2,1)} fusion(f32[384,7168]{1,0:T(8,128)S(1)} %fusion.50, f32[384,7168]{1,0:T(8,128)S(1)} %fusion.51), kind=kLoop, calls=%fused_computation | loop fusion | flops 5505024 | bytes 27525120 | tf_op jit(solution)/shard_map/convert_element_type | solution.py:227
  (158 shorter events, 64.0 us)
Async XLA Ops:
  4.7 28.3 %collective-permute-start.21 = (bf16[192,512]{1,0:T(8,128)(2,1)S(1)}, bf16[192,512]{1,0:T(8,128)(2,1)S(1)}, u32[]{:S(2)}, u32[]{:S(2)}) collective-permute-start(bf16[192,512]{1,0:T(8,128)(2,1)S(1)} %bitcast.169), channel_id=1, source_target_pairs={{0,12},{4,8},{8,4},{12,0},{1,13},{5,9},{9,5},{13,1},{2,14},{6,10},... | collective-permute-start | bytes 589832 | tf_op jit(solution)/shard_map/ppermute | solution.py:83
  9.9 23.3 %collective-permute-start.20 = (bf16[192,512]{1,0:T(8,128)(2,1)S(1)}, bf16[192,512]{1,0:T(8,128)(2,1)S(1)}, u32[]{:S(2)}, u32[]{:S(2)}) collective-permute-start(bf16[192,512]{1,0:T(8,128)(2,1)S(1)} %bitcast.168), channel_id=1, source_target_pairs={{0,8},{4,12},{8,0},{12,4},{1,9},{5,13},{9,1},{13,5},{2,10},{6,14},... | collective-permute-start | bytes 589832 | tf_op jit(solution)/shard_map/ppermute | solution.py:83
  10.0 23.1 %collective-permute-start.19 = (bf16[192,512]{1,0:T(8,128)(2,1)S(1)}, bf16[192,512]{1,0:T(8,128)(2,1)S(1)}, u32[]{:S(2)}, u32[]{:S(2)}) collective-permute-start(bf16[192,512]{1,0:T(8,128)(2,1)S(1)} %bitcast.170), channel_id=1, source_target_pairs={{0,4},{4,0},{8,12},{12,8},{1,5},{5,1},{9,13},{13,9},{2,6},{6,2},{1... | collective-permute-start | bytes 589832 | tf_op jit(solution)/shard_map/ppermute | solution.py:83
  10.6 83.1 %collective-permute-start = (bf16[192,7168]{1,0:T(8,128)(2,1)}, bf16[192,7168]{1,0:T(8,128)(2,1)}, u32[]{:S(2)}, u32[]{:S(2)}) collective-permute-start(bf16[192,7168]{1,0:T(8,128)(2,1)} %param.8), channel_id=1, source_target_pairs={{0,1},{1,0},{2,3},{3,2},{4,5},{5,4},{6,7},{7,6},{8,9},{9,8},{10,11... | collective-permute-start | bytes 8257544 | tf_op jit(solution)/shard_map/ppermute | solution.py:83
  16.2 8.5 %collective-permute-start.5 = (f32[192,64]{0,1:T(8,128)S(1)}, f32[192,64]{0,1:T(8,128)S(1)}, u32[]{:S(2)}, u32[]{:S(2)}) collective-permute-start(f32[192,64]{0,1:T(8,128)S(1)} %fusion.7), channel_id=1, source_target_pairs={{0,4},{4,0},{8,12},{12,8},{1,5},{5,1},{9,13},{13,9},{2,6},{6,2},{1... | collective-permute-start | bytes 147464 | tf_op jit(solution)/shard_map/ppermute | solution.py:83
  31.3 17.7 %collective-permute-start.1 = (bf16[48,7168]{1,0:T(8,128)(2,1)}, bf16[48,7168]{1,0:T(8,128)(2,1)}, u32[]{:S(2)}, u32[]{:S(2)}) collective-permute-start(bf16[48,7168]{1,0:T(8,128)(2,1)} %get-tuple-element.45), channel_id=1, source_target_pairs={{0,2},{1,3},{2,0},{3,1},{4,6},{5,7},{6,4},{7,5},{8,10},{9,11},{10,... | collective-permute-start | bytes 2064392 | tf_op jit(solution)/shard_map/ppermute | solution.py:83
  34.5 16.2 %collective-permute-start.22 = (f32[2,192,64]{1,0,2:T(2,128)S(1)}, f32[2,192,64]{1,0,2:T(2,128)S(1)}, u32[]{:S(2)}, u32[]{:S(2)}) collective-permute-start(f32[2,192,64]{1,0,2:T(2,128)S(1)} %bitcast.171), channel_id=1, source_target_pairs={{0,1},{1,0},{2,3},{3,2},{4,5},{5,4},{6,7},{7,6},{8,9},{9,8},{10,11... | collective-permute-start | bytes 294920 | tf_op jit(solution)/shard_map/ppermute | solution.py:83
  49.0 18.0 %collective-permute-start.2 = (bf16[48,7168]{1,0:T(8,128)(2,1)S(1)}, bf16[48,7168]{1,0:T(8,128)(2,1)S(1)}, u32[]{:S(2)}, u32[]{:S(2)}) collective-permute-start(bf16[48,7168]{1,0:T(8,128)(2,1)S(1)} %get-tuple-element.15), channel_id=1, source_target_pairs={{0,2},{1,3},{2,0},{3,1},{4,6},{5,7},{6,4},{7,5},{8,10},{9,11},{10,... | collective-permute-start | bytes 2064392 | tf_op jit(solution)/shard_map/ppermute | solution.py:83
  51.0 16.0 %collective-permute-start.8 = (bf16[2,192,64]{1,2,0:T(8,128)(2,1)S(1)}, bf16[2,192,64]{1,2,0:T(8,128)(2,1)S(1)}, u32[]{:S(2)}, u32[]{:S(2)}) collective-permute-start(bf16[2,192,64]{1,2,0:T(8,128)(2,1)S(1)} %pad_maximum_fusion.4), channel_id=1, source_target_pairs={{0,2},{1,3},{2,0},{3,1},{4,6},{5,7},{6,4},{7,5},{8,10},{9,11},{10,... | collective-permute-start | bytes 147464 | tf_op jit(solution)/shard_map/ppermute | solution.py:83
  51.4 48.7 %collective-permute-start.3 = (bf16[48,7168]{1,0:T(8,128)(2,1)}, bf16[48,7168]{1,0:T(8,128)(2,1)}, u32[]{:S(2)}, u32[]{:S(2)}) collective-permute-start(bf16[48,7168]{1,0:T(8,128)(2,1)} %collective-permute-done.1), channel_id=1, source_target_pairs={{0,1},{1,0},{2,3},{3,2},{4,5},{5,4},{6,7},{7,6},{8,9},{9,8},{10,11... | collective-permute-start | bytes 2064392 | tf_op jit(solution)/shard_map/ppermute | solution.py:83
  72.5 15.6 %collective-permute-start.15 = (bf16[48,7168]{1,0:T(8,128)(2,1)}, bf16[48,7168]{1,0:T(8,128)(2,1)}, u32[]{:S(2)}, u32[]{:S(2)}) collective-permute-start(bf16[48,7168]{1,0:T(8,128)(2,1)} %get-tuple-element.17), channel_id=1, source_target_pairs={{0,2},{1,3},{2,0},{3,1},{4,6},{5,7},{6,4},{7,5},{8,10},{9,11},{10,... | collective-permute-start | bytes 2064392 | tf_op jit(solution)/shard_map/ppermute | solution.py:83
  83.1 19.0 %collective-permute-start.4 = (bf16[48,7168]{1,0:T(8,128)(2,1)S(1)}, bf16[48,7168]{1,0:T(8,128)(2,1)}, u32[]{:S(2)}, u32[]{:S(2)}) collective-permute-start(bf16[48,7168]{1,0:T(8,128)(2,1)S(1)} %collective-permute-done.2), channel_id=1, source_target_pairs={{0,1},{1,0},{2,3},{3,2},{4,5},{5,4},{6,7},{7,6},{8,9},{9,8},{10,11... | collective-permute-start | bytes 2064392 | tf_op jit(solution)/shard_map/ppermute | solution.py:83
  90.0 38.5 %collective-permute-start.16 = (bf16[48,7168]{1,0:T(8,128)(2,1)}, bf16[48,7168]{1,0:T(8,128)(2,1)}, u32[]{:S(2)}, u32[]{:S(2)}) collective-permute-start(bf16[48,7168]{1,0:T(8,128)(2,1)} %get-tuple-element.18), channel_id=1, source_target_pairs={{0,2},{1,3},{2,0},{3,1},{4,6},{5,7},{6,4},{7,5},{8,10},{9,11},{10,... | collective-permute-start | bytes 2064392 | tf_op jit(solution)/shard_map/ppermute | solution.py:83
  93.2 46.3 %collective-permute-start.17 = (bf16[48,7168]{1,0:T(8,128)(2,1)}, bf16[48,7168]{1,0:T(8,128)(2,1)}, u32[]{:S(2)}, u32[]{:S(2)}) collective-permute-start(bf16[48,7168]{1,0:T(8,128)(2,1)} %collective-permute-done.15), channel_id=1, source_target_pairs={{0,1},{1,0},{2,3},{3,2},{4,5},{5,4},{6,7},{7,6},{8,9},{9,8},{10,11... | collective-permute-start | bytes 2064392 | tf_op jit(solution)/shard_map/ppermute | solution.py:83
  121.9 13.0 %collective-permute-start.9 = (bf16[96,2048]{1,0:T(8,128)(2,1)S(1)}, bf16[96,2048]{1,0:T(8,128)(2,1)S(1)}, u32[]{:S(2)}, u32[]{:S(2)}) collective-permute-start(bf16[96,2048]{1,0:T(8,128)(2,1)S(1)} %get-tuple-element.36), channel_id=1, source_target_pairs={{0,4},{1,5},{2,6},{3,7},{16,20},{17,21},{18,22},{19,23}} | collective-permute-start | bytes 1179656 | tf_op jit(solution)/shard_map/ppermute | solution.py:209
  125.9 15.6 %collective-permute-start.12 = (bf16[96,2048]{1,0:T(8,128)(2,1)S(1)}, bf16[96,2048]{1,0:T(8,128)(2,1)S(1)}, u32[]{:S(2)}, u32[]{:S(2)}) collective-permute-start(bf16[96,2048]{1,0:T(8,128)(2,1)S(1)} %get-tuple-element.35), channel_id=1, source_target_pairs={{12,8},{13,9},{14,10},{15,11},{28,24},{29,25},{30,26},{31,27}} | collective-permute-start | bytes 1179656 | tf_op jit(solution)/shard_map/ppermute | solution.py:210
  128.6 21.7 %collective-permute-start.18 = (bf16[48,7168]{1,0:T(8,128)(2,1)}, bf16[48,7168]{1,0:T(8,128)(2,1)S(1)}, u32[]{:S(2)}, u32[]{:S(2)}) collective-permute-start(bf16[48,7168]{1,0:T(8,128)(2,1)} %collective-permute-done.16), channel_id=1, source_target_pairs={{0,1},{1,0},{2,3},{3,2},{4,5},{5,4},{6,7},{7,6},{8,9},{9,8},{10,11... | collective-permute-start | bytes 2064392 | tf_op jit(solution)/shard_map/ppermute | solution.py:83
  135.0 12.6 %collective-permute-start.10 = (bf16[96,2048]{1,0:T(8,128)(2,1)S(1)}, bf16[96,2048]{1,0:T(8,128)(2,1)S(1)}, u32[]{:S(2)}, u32[]{:S(2)}) collective-permute-start(bf16[96,2048]{1,0:T(8,128)(2,1)S(1)} %fusion.19), channel_id=1, source_target_pairs={{0,4},{4,8},{1,5},{5,9},{2,6},{6,10},{3,7},{7,11},{16,20},{20,24},... | collective-permute-start | bytes 1179656 | tf_op jit(solution)/shard_map/ppermute | solution.py:209
  151.2 50.1 %collective-permute-start.11 = (bf16[96,2048]{1,0:T(8,128)(2,1)}, bf16[96,2048]{1,0:T(8,128)(2,1)S(1)}, u32[]{:S(2)}, u32[]{:S(2)}) collective-permute-start(bf16[96,2048]{1,0:T(8,128)(2,1)} %get-tuple-element.27), channel_id=1, source_target_pairs={{0,4},{4,8},{8,12},{1,5},{5,9},{9,13},{2,6},{6,10},{10,14},{3,7},{... | collective-permute-start | bytes 1179656 | tf_op jit(solution)/shard_map/ppermute | solution.py:209
  175.6 15.8 %collective-permute-start.28 = (bf16[96,2048]{1,0:T(8,128)(2,1)S(1)}, bf16[96,2048]{1,0:T(8,128)(2,1)S(1)}, u32[]{:S(2)}, u32[]{:S(2)}) collective-permute-start(bf16[96,2048]{1,0:T(8,128)(2,1)S(1)} %get-tuple-element.34), channel_id=1, source_target_pairs={{0,4},{1,5},{2,6},{3,7},{16,20},{17,21},{18,22},{19,23}} | collective-permute-start | bytes 1179656 | tf_op jit(solution)/shard_map/ppermute | solution.py:209
  187.1 14.2 %collective-permute-start.14 = (bf16[96,2048]{1,0:T(8,128)(2,1)S(1)}, bf16[96,2048]{1,0:T(8,128)(2,1)S(1)}, u32[]{:S(2)}, u32[]{:S(2)}) collective-permute-start(bf16[96,2048]{1,0:T(8,128)(2,1)S(1)} %fusion.18), channel_id=1, source_target_pairs={{12,8},{8,4},{4,0},{13,9},{9,5},{5,1},{14,10},{10,6},{6,2},{15,11}... | collective-permute-start | bytes 1179656 | tf_op jit(solution)/shard_map/ppermute | solution.py:210
  192.9 9.9 %collective-permute-start.30 = (bf16[96,2048]{1,0:T(8,128)(2,1)S(1)}, bf16[96,2048]{1,0:T(8,128)(2,1)S(1)}, u32[]{:S(2)}, u32[]{:S(2)}) collective-permute-start(bf16[96,2048]{1,0:T(8,128)(2,1)S(1)} %get-tuple-element.32), channel_id=1, source_target_pairs={{0,4},{4,8},{1,5},{5,9},{2,6},{6,10},{3,7},{7,11},{16,20},{20,24},... | collective-permute-start | bytes 1179656 | tf_op jit(solution)/shard_map/ppermute | solution.py:209
  203.2 20.8 %collective-permute-start.33 = (bf16[96,2048]{1,0:T(8,128)(2,1)S(1)}, bf16[96,2048]{1,0:T(8,128)(2,1)S(1)}, u32[]{:S(2)}, u32[]{:S(2)}) collective-permute-start(bf16[96,2048]{1,0:T(8,128)(2,1)S(1)} %get-tuple-element.30), channel_id=1, source_target_pairs={{12,8},{8,4},{4,0},{13,9},{9,5},{5,1},{14,10},{10,6},{6,2},{15,11}... | collective-permute-start | bytes 1179656 | tf_op jit(solution)/shard_map/ppermute | solution.py:210
  204.5 19.5 %collective-permute-start.32 = (bf16[96,2048]{1,0:T(8,128)(2,1)S(1)}, bf16[96,2048]{1,0:T(8,128)(2,1)S(1)}, u32[]{:S(2)}, u32[]{:S(2)}) collective-permute-start(bf16[96,2048]{1,0:T(8,128)(2,1)S(1)} %get-tuple-element.29), channel_id=1, source_target_pairs={{0,4},{4,8},{8,12},{1,5},{5,9},{9,13},{2,6},{6,10},{10,14},{3,7},{... | collective-permute-start | bytes 1179656 | tf_op jit(solution)/shard_map/ppermute | solution.py:209
  (21 other events, 264.7 us)

commit v4 on v3

--- a/solution.py
+++ b/solution.py
@@ -102,15 +102,8 @@
     bf16, f32 = jnp.bfloat16, jnp.float32
 
     mate = swap(grad_out, "tensor", 1, n)
-    legs = 2 * chunks
-    leg_rows = host_rows // legs
-    across, relayed = [], []
-    for c in range(legs):
-        sent = grad_out[c * leg_rows : (c + 1) * leg_rows]
-        if across:
-            sent = after(sent, across[-1])
-        across.append(swap(sent, "tensor", 2, n))
-        relayed.append(swap(across[-1], "tensor", 1, n))
+    first = swap(grad_out[:step_rows], "tensor", 2, n)
+    first_relayed = swap(first, "tensor", 1, n)
 
     by_owner = inputs.reshape(host_rows, n, own_cols).transpose(1, 0, 2)
     kept = take(by_owner, z)
@@ -143,9 +136,9 @@
         value = value + swap(value, "fsdp", 1, n)
         return value + swap(value, "fsdp", 2, n)
 
-    def every_block(value, leg):
+    def every_block(value, earlier):
         pair = jnp.stack([value, swap(value, "tensor", 1, n)])
-        pair = after(pair, across[leg])
+        pair = after(pair, earlier)
         return jnp.concatenate([pair, swap(pair, "tensor", 2, n)], axis=0)
 
     own_member = take(member_blocks, t)
@@ -153,17 +146,13 @@
         lax.dot_general(grad_out, b_flat, (((1,), (1,)), ((), ())), preferred_element_type=f32),
         own_member,
     )
-    grad_order = every_block(doubled(grad_part).astype(bf16), 0)
+    grad_order = every_block(doubled(grad_part).astype(bf16), first)
+    second = swap(after(grad_out[step_rows:], grad_order), "tensor", 2, n)
     low_grad = ordered(grad_order, t).reshape(total_rows, rank_dim)
 
     rows_in = ordered(rows_in, z).reshape(total_rows, own_cols)
     in_part = pick(jnp.dot(rows_in, a_flat, preferred_element_type=f32), member)
     by_core = in_part.reshape(2, 2, host_rows, rank_dim).transpose(1, 0, 2, 3)
-    halves = take(by_core, t % 2) + swap(take(by_core, 1 - t % 2), "tensor", 1, n)
-    other = after(take(halves, 1 - t // 2), across[1])
-    own_in = take(halves, t // 2) + swap(other, "tensor", 2, n)
-    in_order = every_block(doubled(own_in).astype(bf16), 2)
-
     spread_grad = spread(low_grad, member)
     grad_a = lax.dot_general(
         spread_grad, rows_in, (((0,), (0,)), ((), ())), preferred_element_type=f32
@@ -181,25 +170,26 @@
     finished, passed, operands = [], [], []
     for c in range(chunks):
         rows = slice(c * step_rows, (c + 1) * step_rows)
-        here = slice(2 * c, 2 * c + 2)
-        gathered = jnp.concatenate(
-            [grad_out[rows], mate[rows]] + across[here] + relayed[here], axis=0
-        )
+        across, relayed = (first, first_relayed) if c == 0 else (second, second_relayed)
+        gathered = jnp.concatenate([grad_out[rows], mate[rows], across, relayed], axis=0)
         if passed:
             gathered = after(gathered, passed[n - 3])
         part = lax.dot_general(
             gathered, base_weight, (((1,), (1,)), ((), ())), preferred_element_type=f32
         ).astype(bf16).reshape(n, step_rows, feature_cols)
 
-        def own(dest):
+        def own(dest, rows=rows, part=part):
             dest = jnp.clip(dest, 0, n - 1)
             return take(part, dest ^ t).astype(f32) + take(low_rank[:, rows], dest).astype(f32)
 
-        spread_in = spread(
-            in_order[:, rows].reshape(n * step_rows, rank_dim),
-            member_order[:, rows].reshape(n * step_rows, adapters),
-        )
-        operands.append((spread_in, gathered))
+        operands.append(gathered)
+        if c == 0:
+            second_relayed = swap(after(second, part), "tensor", 1, n)
+            halves = after(by_core, (second, part))
+            halves = take(halves, t % 2) + swap(take(halves, 1 - t % 2), "tensor", 1, n)
+            own_in = take(halves, t // 2) + swap(take(halves, 1 - t // 2), "tensor", 2, n)
+            own_in = doubled(own_in).astype(bf16)
+            in_order = every_block(own_in, part)
         up = down = None
         passed = []
         for k in range(1, n):
@@ -211,10 +201,14 @@
                 to_down.astype(bf16), "fsdp", [(n - 1 - i, n - 2 - i) for i in range(k)]
             )
             if c == chunks - 1 and k > 1:
-                spread_in, gathered = operands[k - 2]
+                rows = slice((k - 2) * step_rows, (k - 1) * step_rows)
+                spread_in = spread(
+                    in_order[:, rows].reshape(n * step_rows, rank_dim),
+                    member_order[:, rows].reshape(n * step_rows, adapters),
+                )
                 term = lax.dot_general(
                     after(spread_in, passed[-1]),
-                    gathered,
+                    operands[k - 2],
                     (((0,), (0,)), ((), ())),
                     preferred_element_type=f32,
                 )

time: 226 us -> 195 us (0.86)
  local copies, waits for them, and re-layouts: 32.2 us -> 12.1 us
  waiting for transfers between devices: 62.1 us -> 51.9 us
  starting transfers between devices: 65.3 us -> 56.9 us
  other arithmetic: 12.6 us -> 19.8 us
    unnamed x39 -> x45, local copies, waits for them, and re-layouts: 18.1 us -> 1.17 us
    ppermute x22 -> x18, waiting for transfers between devices: 48.6 us -> 36.8 us  [swap(): return lax.ppermute(value, axis, [(i, i ^ mask) for i in range(count)])]
    ppermute x6, starting transfers between devices: 37.9 us -> 32 us  [body4(): lax.ppermute(to_up.astype(bf16), 'fsdp', [(i, i + 1) for i in range(k)])]
    concatenate x0 -> x1, other arithmetic: none -> 3.54 us  [body4(): jnp.concatenate([grad_out[rows], mate[rows], across, relayed], axis=0)]
    concatenate x2 -> x0, local copies, waits for them, and re-layouts: 2.89 us -> none  [body4(): jnp.concatenate([grad_out[rows], mate[rows]] + across[here] + relayed[her...]
    ppermute x6, waiting for transfers between devices: 0.02 us -> 2.58 us  [body4(): lax.ppermute(to_down.astype(bf16), 'fsdp', [(n - 1 - i, n - 2 - i) for i...]
    ppermute x22 -> x18, starting transfers between devices: 21.2 us -> 19.5 us  [swap(): return lax.ppermute(value, axis, [(i, i ^ mask) for i in range(count)])]
  transfers between devices with their start and end apart: 34 -> 30, of which waited for: 12 -> 15; matrix products, arithmetic and copies ran while one was open for 40% -> 41% of each run, Pallas kernels for 0% -> 0%
where the time goes in v4:
time: 195 us; the launch traced here: 194 us
  starting transfers between devices  56.9 us (29%)
  waiting for transfers between devices  51.9 us (27%)
  matrix products  51.7 us (27%)
  other arithmetic  19.8 us (10%)
  local copies, waits for them, and re-layouts  12.1 us (6%)
    ppermute x18, waiting for transfers between devices, swap(): return lax.ppermute(value, axis, [(i, i ^ mask) for i in range(count)])  36.8 us
    dot_general x2, matrix products, body4(): lax.dot_general(gathered, base_weight, (((1,), (1,)), ((), ())), preferre...  35.6 us
    ppermute x6, starting transfers between devices, body4(): lax.ppermute(to_up.astype(bf16), 'fsdp', [(i, i + 1) for i in range(k)])  32 us
    ppermute x18, starting transfers between devices, swap(): return lax.ppermute(value, axis, [(i, i ^ mask) for i in range(count)])  19.5 us
    ppermute x6, waiting for transfers between devices, body4(): lax.ppermute(to_up.astype(bf16), 'fsdp', [(i, i + 1) for i in range(k)])  12.5 us
    dot_general x2, matrix products, body4(): lax.dot_general(after(spread_in, passed[-1]), operands[k - 2], (((0,), (0...  7.83 us
    ppermute x6, starting transfers between devices, body4(): lax.ppermute(to_down.astype(bf16), 'fsdp', [(n - 1 - i, n - 2 - i) for i...  5.42 us
    dot_general x1, matrix products, body4(): lax.dot_general(grad_out, b_flat, (((1,), (1,)), ((), ())), preferred_ele...  5.07 us
  transfers between devices with their start and end apart: 30, of which 15 were waited for; matrix products, arithmetic and copies ran while one was open for 41% of the time, Pallas kernels for 0%

profile of v4, /device:TPU:0, one launch (start us, length us, event | category | flops | bytes accessed | tf_op | source)
XLA Modules:
  0.0 193.9 jit_solution(8341444856768507304)
XLA Ops:
  3.0 5.1 %fusion.7 = f32[192,64]{0,1:T(8,128)S(1)} fusion(bf16[6,64,7168]{2,1,0:T(8,128)(2,1)} %param.11, bf16[192,7168]{1,0:T(8,128)(2,1)} %param.8, f32[192,6]{0,1:T(8,128)S(1)} %bitcast.175), kind=kOutput, calls=%fused_computation.13 | convolution fusion | flops 1057099776 | bytes 8311296 | tf_op jit(solution)/shard_map/dot_general | solution.py:146
  8.1 2.7 %collective-permute-start.3 = (f32[192,64]{0,1:T(8,128)S(1)}, f32[192,64]{0,1:T(8,128)S(1)}, u32[]{:S(2)}, u32[]{:S(2)}) collective-permute-start(f32[192,64]{0,1:T(8,128)S(1)} %fusion.7), channel_id=1, source_target_pairs={{0,4},{4,0},{8,12},{12,8},{1,5},{5,1},{9,13},{13,9},{2,6},{6,2},{1... | collective-permute-start | bytes 147464 | tf_op jit(solution)/shard_map/ppermute | solution.py:83
  13.2 3.1 %collective-permute-start.16 = (bf16[192,512]{1,0:T(8,128)(2,1)S(1)}, bf16[192,512]{1,0:T(8,128)(2,1)S(1)}, u32[]{:S(2)}, u32[]{:S(2)}) collective-permute-start(bf16[192,512]{1,0:T(8,128)(2,1)S(1)} %bitcast.167), channel_id=1, source_target_pairs={{0,8},{4,12},{8,0},{12,4},{1,9},{5,13},{9,1},{13,5},{2,10},{6,14},... | collective-permute-start | bytes 589832 | tf_op jit(solution)/shard_map/ppermute | solution.py:83
  21.1 8.1 %collective-permute-done.4 = f32[192,64]{0,1:T(8,128)S(1)} collective-permute-done((f32[192,64]{0,1:T(8,128)S(1)}, f32[192,64]{0,1:T(8,128)S(1)}, u32[]{:S(2)}, u32[]{:S(2)}) %collective-permute-start.4) | collective-permute-done | bytes 49184 | tf_op jit(solution)/shard_map/ppermute | solution.py:83
  30.5 2.8 %collective-permute-start.17 = (bf16[192,512]{1,0:T(8,128)(2,1)S(1)}, bf16[192,512]{1,0:T(8,128)(2,1)S(1)}, u32[]{:S(2)}, u32[]{:S(2)}) collective-permute-start(bf16[192,512]{1,0:T(8,128)(2,1)S(1)} %bitcast.168), channel_id=1, source_target_pairs={{0,12},{4,8},{8,4},{12,0},{1,13},{5,9},{9,5},{13,1},{2,14},{6,10},... | collective-permute-start | bytes 589832 | tf_op jit(solution)/shard_map/ppermute | solution.py:83
  34.5 4.9 %collective-permute-done.17 = bf16[192,512]{1,0:T(8,128)(2,1)S(1)} collective-permute-done((bf16[192,512]{1,0:T(8,128)(2,1)S(1)}, bf16[192,512]{1,0:T(8,128)(2,1)S(1)}, u32[]{:S(2)}, u32[]{:S(2)}) %collective-permute-start.17) | collective-permute-done | bytes 196640 | tf_op jit(solution)/shard_map/ppermute | solution.py:83
  42.1 7.5 %collective-permute-done.1 = bf16[96,7168]{1,0:T(8,128)(2,1)} collective-permute-done((bf16[96,7168]{1,0:T(8,128)(2,1)}, bf16[96,7168]{1,0:T(8,128)(2,1)}, u32[]{:S(2)}, u32[]{:S(2)}) %collective-permute-start.1) | collective-permute-done | bytes 1376288 | tf_op jit(solution)/shard_map/ppermute | solution.py:83
  51.1 2.8 %collective-permute-done.6 = bf16[2,192,64]{1,2,0:T(8,128)(2,1)S(1)} collective-permute-done((bf16[2,192,64]{1,2,0:T(8,128)(2,1)S(1)}, bf16[2,192,64]{1,2,0:T(8,128)(2,1)S(1)}, u32[]{:S(2)}, u32[]{:S(2)}) %collective-permute-start.6) | collective-permute-done | bytes 49184 | tf_op jit(solution)/shard_map/ppermute | solution.py:83
  55.4 3.0 %fusion.50 = (bf16[96,7168]{1,0:T(8,128)(2,1)}, bf16[96,7168]{1,0:T(8,128)(2,1)S(1)}) fusion(bf16[192,7168]{1,0:T(8,128)(2,1)} %collective-permute-done), kind=kLoop, calls=%fused_computation.119 | loop fusion | bytes 5505024 | tf_op jit(solution)/shard_map/slice | solution.py:174
  58.4 18.9 %convolution_convert_fusion.1 = bf16[384,2048]{1,0:T(8,128)(2,1)} fusion(bf16[2048,7168]{1,0:T(8,128)(2,1)} %param.9, bf16[96,7168]{1,0:T(8,128)(2,1)} %collective-permute-done.2, bf16[96,7168]{1,0:T(8,128)(2,1)} %collective-permute-done.1, bf16[96,7168]{1,0:T(8,128)(2,1)S(1)} %get-tuple-element.38, bf16[96,7168]{1,0:T(8,128)(2,1)} %get-tuple-element.39), kind=kOutput, calls=%fused_computation.4 | convolution fusion | flops 11297095680 | bytes 36438016 | tf_op jit(solution)/shard_map/dot_general | solution.py:177
  77.4 6.5 %collective-permute-done.13 = bf16[96,7168]{1,0:T(8,128)(2,1)} collective-permute-done((bf16[96,7168]{1,0:T(8,128)(2,1)S(1)}, bf16[96,7168]{1,0:T(8,128)(2,1)}, u32[]{:S(2)}, u32[]{:S(2)}) %collective-permute-start.13) | collective-permute-done | bytes 1376288 | tf_op jit(solution)/shard_map/ppermute | solution.py:83
  95.2 4.0 %collective-permute-start.7 = (bf16[96,2048]{1,0:T(8,128)(2,1)S(1)}, bf16[96,2048]{1,0:T(8,128)(2,1)S(1)}, u32[]{:S(2)}, u32[]{:S(2)}) collective-permute-start(bf16[96,2048]{1,0:T(8,128)(2,1)S(1)} %get-tuple-element.34), channel_id=1, source_target_pairs={{0,4},{1,5},{2,6},{3,7},{16,20},{17,21},{18,22},{19,23}} | collective-permute-start | bytes 1179656 | tf_op jit(solution)/shard_map/ppermute | solution.py:199
  105.3 4.4 %collective-permute-start.8 = (bf16[96,2048]{1,0:T(8,128)(2,1)S(1)}, bf16[96,2048]{1,0:T(8,128)(2,1)S(1)}, u32[]{:S(2)}, u32[]{:S(2)}) collective-permute-start(bf16[96,2048]{1,0:T(8,128)(2,1)S(1)} %fusion.20), channel_id=1, source_target_pairs={{0,4},{4,8},{1,5},{5,9},{2,6},{6,10},{3,7},{7,11},{16,20},{20,24},... | collective-permute-start | bytes 1179656 | tf_op jit(solution)/shard_map/ppermute | solution.py:199
  110.2 6.1 %collective-permute-done.8 = bf16[96,2048]{1,0:T(8,128)(2,1)S(1)} collective-permute-done((bf16[96,2048]{1,0:T(8,128)(2,1)S(1)}, bf16[96,2048]{1,0:T(8,128)(2,1)S(1)}, u32[]{:S(2)}, u32[]{:S(2)}) %collective-permute-start.8) | collective-permute-done | bytes 393248 | tf_op jit(solution)/shard_map/ppermute | solution.py:199
  120.3 5.0 %collective-permute-start.9 = (bf16[96,2048]{1,0:T(8,128)(2,1)}, bf16[96,2048]{1,0:T(8,128)(2,1)S(1)}, u32[]{:S(2)}, u32[]{:S(2)}) collective-permute-start(bf16[96,2048]{1,0:T(8,128)(2,1)} %get-tuple-element.25), channel_id=1, source_target_pairs={{0,4},{4,8},{8,12},{1,5},{5,9},{9,13},{2,6},{6,10},{10,14},{3,7},{... | collective-permute-start | bytes 1179656 | tf_op jit(solution)/shard_map/ppermute | solution.py:199
  128.6 3.5 %pad_maximum_fusion.1 = bf16[384,7168]{1,0:T(8,128)(2,1)S(1)} fusion(bf16[96,7168]{1,0:T(8,128)(2,1)} %collective-permute-done.14, bf16[96,7168]{1,0:T(8,128)(2,1)} %collective-permute-done.13, bf16[96,7168]{1,0:T(8,128)(2,1)} %get-tuple-element.37, bf16[96,7168]{1,0:T(8,128)(2,1)} %copy-done.3), kind=kLoop, calls=%fused_computation.2 | loop fusion | flops 22020096 | bytes 11010048 | tf_op jit(solution)/shard_map/concatenate | solution.py:174
  132.2 16.7 %convolution_convert_fusion = bf16[384,2048]{1,0:T(8,128)(2,1)} fusion(bf16[384,7168]{1,0:T(8,128)(2,1)S(1)} %pad_maximum_fusion.1, bf16[2048,7168]{1,0:T(8,128)(2,1)} %param.9), kind=kOutput, calls=%fused_computation.3 | convolution fusion | flops 11275075584 | bytes 36438016 | tf_op jit(solution)/shard_map/dot_general | solution.py:177
  151.2 8.6 %collective-permute-start.24 = (bf16[96,2048]{1,0:T(8,128)(2,1)S(1)}, bf16[96,2048]{1,0:T(8,128)(2,1)S(1)}, u32[]{:S(2)}, u32[]{:S(2)}) collective-permute-start(bf16[96,2048]{1,0:T(8,128)(2,1)S(1)} %get-tuple-element.32), channel_id=1, source_target_pairs={{0,4},{1,5},{2,6},{3,7},{16,20},{17,21},{18,22},{19,23}} | collective-permute-start | bytes 1179656 | tf_op jit(solution)/shard_map/ppermute | solution.py:199
  161.3 3.9 %collective-permute-done.24 = bf16[96,2048]{1,0:T(8,128)(2,1)S(1)} collective-permute-done((bf16[96,2048]{1,0:T(8,128)(2,1)S(1)}, bf16[96,2048]{1,0:T(8,128)(2,1)S(1)}, u32[]{:S(2)}, u32[]{:S(2)}) %collective-permute-start.24) | collective-permute-done | bytes 393248 | tf_op jit(solution)/shard_map/ppermute | solution.py:199
  166.2 5.0 %collective-permute-start.26 = (bf16[96,2048]{1,0:T(8,128)(2,1)S(1)}, bf16[96,2048]{1,0:T(8,128)(2,1)S(1)}, u32[]{:S(2)}, u32[]{:S(2)}) collective-permute-start(bf16[96,2048]{1,0:T(8,128)(2,1)S(1)} %get-tuple-element.30), channel_id=1, source_target_pairs={{0,4},{4,8},{1,5},{5,9},{2,6},{6,10},{3,7},{7,11},{16,20},{20,24},... | collective-permute-start | bytes 1179656 | tf_op jit(solution)/shard_map/ppermute | solution.py:199
  171.3 4.8 %fusion.10 = f32[384,7168]{1,0:T(8,128)S(1)} fusion(bf16[384,384]{0,1:T(8,128)(2,1)S(1)} %bitcast.162, bf16[96,7168]{1,0:T(8,128)(2,1)} %collective-permute-done.2, bf16[96,7168]{1,0:T(8,128)(2,1)} %collective-permute-done.1, bf16[96,7168]{1,0:T(8,128)(2,1)S(1)} %copy-done.8, bf16[96,7168]{1,0:T(8,128)(2,1)} %get-tuple-element.39), kind=kOutput, calls=%fused_computation.14 | convolution fusion | flops 2135949312 | bytes 16809984 | tf_op jit(solution)/shard_map/dot_general | solution.py:209
  177.6 4.9 %collective-permute-start.28 = (bf16[96,2048]{1,0:T(8,128)(2,1)S(1)}, bf16[96,2048]{1,0:T(8,128)(2,1)S(1)}, u32[]{:S(2)}, u32[]{:S(2)}) collective-permute-start(bf16[96,2048]{1,0:T(8,128)(2,1)S(1)} %get-tuple-element.27), channel_id=1, source_target_pairs={{0,4},{4,8},{8,12},{1,5},{5,9},{9,13},{2,6},{6,10},{10,14},{3,7},{... | collective-permute-start | bytes 1179656 | tf_op jit(solution)/shard_map/ppermute | solution.py:199
  183.8 3.0 %fusion.54 = f32[384,7168]{1,0:T(8,128)S(1)} fusion(bf16[384,384]{0,1:T(8,128)(2,1)S(1)} %bitcast.157, bf16[384,7168]{1,0:T(8,128)(2,1)S(1)} %pad_maximum_fusion.1), kind=kOutput, calls=%fused_computation.123 | convolution fusion | flops 2113929216 | bytes 16809984 | tf_op jit(solution)/shard_map/dot_general | solution.py:209
  186.9 3.2 %add_convert_fusion = bf16[384,7168]{1,0:T(8,128)(2,1)} fusion(f32[384,7168]{1,0:T(8,128)S(1)} %fusion.10, f32[384,7168]{1,0:T(8,128)S(1)} %fusion.54), kind=kLoop, calls=%fused_computation | loop fusion | flops 5505024 | bytes 27525120 | tf_op jit(solution)/shard_map/convert_element_type | solution.py:221
  (155 shorter events, 53.8 us)
Async XLA Ops:
  0.6 54.7 %collective-permute-start = (bf16[192,7168]{1,0:T(8,128)(2,1)}, bf16[192,7168]{1,0:T(8,128)(2,1)}, u32[]{:S(2)}, u32[]{:S(2)}) collective-permute-start(bf16[192,7168]{1,0:T(8,128)(2,1)} %param.8), channel_id=1, source_target_pairs={{0,1},{1,0},{2,3},{3,2},{4,5},{5,4},{6,7},{7,6},{8,9},{9,8},{10,11... | collective-permute-start | bytes 8257544 | tf_op jit(solution)/shard_map/ppermute | solution.py:83
  8.1 12.5 %collective-permute-start.3 = (f32[192,64]{0,1:T(8,128)S(1)}, f32[192,64]{0,1:T(8,128)S(1)}, u32[]{:S(2)}, u32[]{:S(2)}) collective-permute-start(f32[192,64]{0,1:T(8,128)S(1)} %fusion.7), channel_id=1, source_target_pairs={{0,4},{4,0},{8,12},{12,8},{1,5},{5,1},{9,13},{13,9},{2,6},{6,2},{1... | collective-permute-start | bytes 147464 | tf_op jit(solution)/shard_map/ppermute | solution.py:83
  13.1 21.4 %collective-permute-start.15 = (bf16[192,512]{1,0:T(8,128)(2,1)S(1)}, bf16[192,512]{1,0:T(8,128)(2,1)S(1)}, u32[]{:S(2)}, u32[]{:S(2)}) collective-permute-start(bf16[192,512]{1,0:T(8,128)(2,1)S(1)} %bitcast.166), channel_id=1, source_target_pairs={{0,4},{4,0},{8,12},{12,8},{1,5},{5,1},{9,13},{13,9},{2,6},{6,2},{1... | collective-permute-start | bytes 589832 | tf_op jit(solution)/shard_map/ppermute | solution.py:83
  13.2 21.3 %collective-permute-start.16 = (bf16[192,512]{1,0:T(8,128)(2,1)S(1)}, bf16[192,512]{1,0:T(8,128)(2,1)S(1)}, u32[]{:S(2)}, u32[]{:S(2)}) collective-permute-start(bf16[192,512]{1,0:T(8,128)(2,1)S(1)} %bitcast.167), channel_id=1, source_target_pairs={{0,8},{4,12},{8,0},{12,4},{1,9},{5,13},{9,1},{13,5},{2,10},{6,14},... | collective-permute-start | bytes 589832 | tf_op jit(solution)/shard_map/ppermute | solution.py:83
  17.6 32.0 %collective-permute-start.1 = (bf16[96,7168]{1,0:T(8,128)(2,1)}, bf16[96,7168]{1,0:T(8,128)(2,1)}, u32[]{:S(2)}, u32[]{:S(2)}) collective-permute-start(bf16[96,7168]{1,0:T(8,128)(2,1)} %get-tuple-element.39), channel_id=1, source_target_pairs={{0,2},{1,3},{2,0},{3,1},{4,6},{5,7},{6,4},{7,5},{8,10},{9,11},{10,... | collective-permute-start | bytes 4128776 | tf_op jit(solution)/shard_map/ppermute | solution.py:83
  20.6 8.6 %collective-permute-start.4 = (f32[192,64]{0,1:T(8,128)S(1)}, f32[192,64]{0,1:T(8,128)S(1)}, u32[]{:S(2)}, u32[]{:S(2)}) collective-permute-start(f32[192,64]{0,1:T(8,128)S(1)} %add.289), channel_id=1, source_target_pairs={{0,8},{4,12},{8,0},{12,4},{1,9},{5,13},{9,1},{13,5},{2,10},{6,14},... | collective-permute-start | bytes 147464 | tf_op jit(solution)/shard_map/ppermute | solution.py:83
  30.5 8.9 %collective-permute-start.17 = (bf16[192,512]{1,0:T(8,128)(2,1)S(1)}, bf16[192,512]{1,0:T(8,128)(2,1)S(1)}, u32[]{:S(2)}, u32[]{:S(2)}) collective-permute-start(bf16[192,512]{1,0:T(8,128)(2,1)S(1)} %bitcast.168), channel_id=1, source_target_pairs={{0,12},{4,8},{8,4},{12,0},{1,13},{5,9},{9,5},{13,1},{2,14},{6,10},... | collective-permute-start | bytes 589832 | tf_op jit(solution)/shard_map/ppermute | solution.py:83
  51.1 7.3 %collective-permute-start.2 = (bf16[96,7168]{1,0:T(8,128)(2,1)}, bf16[96,7168]{1,0:T(8,128)(2,1)}, u32[]{:S(2)}, u32[]{:S(2)}) collective-permute-start(bf16[96,7168]{1,0:T(8,128)(2,1)} %collective-permute-done.1), channel_id=1, source_target_pairs={{0,1},{1,0},{2,3},{3,2},{4,5},{5,4},{6,7},{7,6},{8,9},{9,8},{10,11... | collective-permute-start | bytes 4128776 | tf_op jit(solution)/shard_map/ppermute | solution.py:83
  53.9 30.0 %collective-permute-start.13 = (bf16[96,7168]{1,0:T(8,128)(2,1)S(1)}, bf16[96,7168]{1,0:T(8,128)(2,1)}, u32[]{:S(2)}, u32[]{:S(2)}) collective-permute-start(bf16[96,7168]{1,0:T(8,128)(2,1)S(1)} %get-tuple-element.15), channel_id=1, source_target_pairs={{0,2},{1,3},{2,0},{3,1},{4,6},{5,7},{6,4},{7,5},{8,10},{9,11},{10,... | collective-permute-start | bytes 4128776 | tf_op jit(solution)/shard_map/ppermute | solution.py:83
  94.5 5.2 %collective-permute-start.21 = (f32[192,64]{0,1:T(8,128)S(1)}, f32[192,64]{0,1:T(8,128)S(1)}, u32[]{:S(2)}, u32[]{:S(2)}) collective-permute-start(f32[192,64]{0,1:T(8,128)S(1)} %add.337), channel_id=1, source_target_pairs={{0,8},{4,12},{8,0},{12,4},{1,9},{5,13},{9,1},{13,5},{2,10},{6,14},... | collective-permute-start | bytes 147464 | tf_op jit(solution)/shard_map/ppermute | solution.py:83
  95.2 9.9 %collective-permute-start.7 = (bf16[96,2048]{1,0:T(8,128)(2,1)S(1)}, bf16[96,2048]{1,0:T(8,128)(2,1)S(1)}, u32[]{:S(2)}, u32[]{:S(2)}) collective-permute-start(bf16[96,2048]{1,0:T(8,128)(2,1)S(1)} %get-tuple-element.34), channel_id=1, source_target_pairs={{0,4},{1,5},{2,6},{3,7},{16,20},{17,21},{18,22},{19,23}} | collective-permute-start | bytes 1179656 | tf_op jit(solution)/shard_map/ppermute | solution.py:199
  101.2 9.0 %collective-permute-start.10 = (bf16[96,2048]{1,0:T(8,128)(2,1)S(1)}, bf16[96,2048]{1,0:T(8,128)(2,1)S(1)}, u32[]{:S(2)}, u32[]{:S(2)}) collective-permute-start(bf16[96,2048]{1,0:T(8,128)(2,1)S(1)} %get-tuple-element.33), channel_id=1, source_target_pairs={{12,8},{13,9},{14,10},{15,11},{28,24},{29,25},{30,26},{31,27}} | collective-permute-start | bytes 1179656 | tf_op jit(solution)/shard_map/ppermute | solution.py:200
  101.9 26.8 %collective-permute-start.14 = (bf16[96,7168]{1,0:T(8,128)(2,1)}, bf16[96,7168]{1,0:T(8,128)(2,1)}, u32[]{:S(2)}, u32[]{:S(2)}) collective-permute-start(bf16[96,7168]{1,0:T(8,128)(2,1)} %collective-permute-done.13), channel_id=1, source_target_pairs={{0,1},{1,0},{2,3},{3,2},{4,5},{5,4},{6,7},{7,6},{8,9},{9,8},{10,11... | collective-permute-start | bytes 4128776 | tf_op jit(solution)/shard_map/ppermute | solution.py:83
  102.5 7.3 %collective-permute-start.23 = (bf16[2,192,64]{1,2,0:T(8,128)(2,1)S(1)}, bf16[2,192,64]{1,2,0:T(8,128)(2,1)S(1)}, u32[]{:S(2)}, u32[]{:S(2)}) collective-permute-start(bf16[2,192,64]{1,2,0:T(8,128)(2,1)S(1)} %pad_maximum_fusion.9), channel_id=1, source_target_pairs={{0,2},{1,3},{2,0},{3,1},{4,6},{5,7},{6,4},{7,5},{8,10},{9,11},{10,... | collective-permute-start | bytes 147464 | tf_op jit(solution)/shard_map/ppermute | solution.py:83
  105.3 11.0 %collective-permute-start.8 = (bf16[96,2048]{1,0:T(8,128)(2,1)S(1)}, bf16[96,2048]{1,0:T(8,128)(2,1)S(1)}, u32[]{:S(2)}, u32[]{:S(2)}) collective-permute-start(bf16[96,2048]{1,0:T(8,128)(2,1)S(1)} %fusion.20), channel_id=1, source_target_pairs={{0,4},{4,8},{1,5},{5,9},{2,6},{6,10},{3,7},{7,11},{16,20},{20,24},... | collective-permute-start | bytes 1179656 | tf_op jit(solution)/shard_map/ppermute | solution.py:199
  118.8 6.5 %collective-permute-start.11 = (bf16[96,2048]{1,0:T(8,128)(2,1)S(1)}, bf16[96,2048]{1,0:T(8,128)(2,1)S(1)}, u32[]{:S(2)}, u32[]{:S(2)}) collective-permute-start(bf16[96,2048]{1,0:T(8,128)(2,1)S(1)} %get-tuple-element.26), channel_id=1, source_target_pairs={{12,8},{8,4},{13,9},{9,5},{14,10},{10,6},{15,11},{11,7},{28,24},{2... | collective-permute-start | bytes 1179656 | tf_op jit(solution)/shard_map/ppermute | solution.py:200
  120.3 39.6 %collective-permute-start.9 = (bf16[96,2048]{1,0:T(8,128)(2,1)}, bf16[96,2048]{1,0:T(8,128)(2,1)S(1)}, u32[]{:S(2)}, u32[]{:S(2)}) collective-permute-start(bf16[96,2048]{1,0:T(8,128)(2,1)} %get-tuple-element.25), channel_id=1, source_target_pairs={{0,4},{4,8},{8,12},{1,5},{5,9},{9,13},{2,6},{6,10},{10,14},{3,7},{... | collective-permute-start | bytes 1179656 | tf_op jit(solution)/shard_map/ppermute | solution.py:199
  127.4 32.5 %collective-permute-start.12 = (bf16[96,2048]{1,0:T(8,128)(2,1)}, bf16[96,2048]{1,0:T(8,128)(2,1)S(1)}, u32[]{:S(2)}, u32[]{:S(2)}) collective-permute-start(bf16[96,2048]{1,0:T(8,128)(2,1)} %fusion.19), channel_id=1, source_target_pairs={{12,8},{8,4},{4,0},{13,9},{9,5},{5,1},{14,10},{10,6},{6,2},{15,11}... | collective-permute-start | bytes 1179656 | tf_op jit(solution)/shard_map/ppermute | solution.py:200
  150.4 10.9 %collective-permute-start.25 = (bf16[96,2048]{1,0:T(8,128)(2,1)S(1)}, bf16[96,2048]{1,0:T(8,128)(2,1)S(1)}, u32[]{:S(2)}, u32[]{:S(2)}) collective-permute-start(bf16[96,2048]{1,0:T(8,128)(2,1)S(1)} %get-tuple-element.31), channel_id=1, source_target_pairs={{12,8},{13,9},{14,10},{15,11},{28,24},{29,25},{30,26},{31,27}} | collective-permute-start | bytes 1179656 | tf_op jit(solution)/shard_map/ppermute | solution.py:200
  151.2 13.9 %collective-permute-start.24 = (bf16[96,2048]{1,0:T(8,128)(2,1)S(1)}, bf16[96,2048]{1,0:T(8,128)(2,1)S(1)}, u32[]{:S(2)}, u32[]{:S(2)}) collective-permute-start(bf16[96,2048]{1,0:T(8,128)(2,1)S(1)} %get-tuple-element.32), channel_id=1, source_target_pairs={{0,4},{1,5},{2,6},{3,7},{16,20},{17,21},{18,22},{19,23}} | collective-permute-start | bytes 1179656 | tf_op jit(solution)/shard_map/ppermute | solution.py:199
  165.5 10.6 %collective-permute-start.27 = (bf16[96,2048]{1,0:T(8,128)(2,1)S(1)}, bf16[96,2048]{1,0:T(8,128)(2,1)S(1)}, u32[]{:S(2)}, u32[]{:S(2)}) collective-permute-start(bf16[96,2048]{1,0:T(8,128)(2,1)S(1)} %get-tuple-element.29), channel_id=1, source_target_pairs={{12,8},{8,4},{13,9},{9,5},{14,10},{10,6},{15,11},{11,7},{28,24},{2... | collective-permute-start | bytes 1179656 | tf_op jit(solution)/shard_map/ppermute | solution.py:200
  166.2 11.0 %collective-permute-start.26 = (bf16[96,2048]{1,0:T(8,128)(2,1)S(1)}, bf16[96,2048]{1,0:T(8,128)(2,1)S(1)}, u32[]{:S(2)}, u32[]{:S(2)}) collective-permute-start(bf16[96,2048]{1,0:T(8,128)(2,1)S(1)} %get-tuple-element.30), channel_id=1, source_target_pairs={{0,4},{4,8},{1,5},{5,9},{2,6},{6,10},{3,7},{7,11},{16,20},{20,24},... | collective-permute-start | bytes 1179656 | tf_op jit(solution)/shard_map/ppermute | solution.py:199
  177.6 12.5 %collective-permute-start.28 = (bf16[96,2048]{1,0:T(8,128)(2,1)S(1)}, bf16[96,2048]{1,0:T(8,128)(2,1)S(1)}, u32[]{:S(2)}, u32[]{:S(2)}) collective-permute-start(bf16[96,2048]{1,0:T(8,128)(2,1)S(1)} %get-tuple-element.27), channel_id=1, source_target_pairs={{0,4},{4,8},{8,12},{1,5},{5,9},{9,13},{2,6},{6,10},{10,14},{3,7},{... | collective-permute-start | bytes 1179656 | tf_op jit(solution)/shard_map/ppermute | solution.py:199
  182.5 10.1 %collective-permute-start.29 = (bf16[96,2048]{1,0:T(8,128)(2,1)S(1)}, bf16[96,2048]{1,0:T(8,128)(2,1)S(1)}, u32[]{:S(2)}, u32[]{:S(2)}) collective-permute-start(bf16[96,2048]{1,0:T(8,128)(2,1)S(1)} %get-tuple-element.28), channel_id=1, source_target_pairs={{12,8},{8,4},{4,0},{13,9},{9,5},{5,1},{14,10},{10,6},{6,2},{15,11}... | collective-permute-start | bytes 1179656 | tf_op jit(solution)/shard_map/ppermute | solution.py:200
  (24 other events, 262.3 us)
